TPU v7x, 128 devices: a whole 4x4x4 slice. The times are simulated.
128 devices in a mesh: row: 8 (over y, core), col: 16 (over x, z).
Axes of the slice: x: 4, y: 4, z: 4, core: 2. Of those that a mesh axis runs over, the one named last changes fastest.
Arguments:
- queries: bfloat16 [16, 16, 128, 1408], P('row', 'col'), may hold values from -240 to 240
- keys: bfloat16 [16, 16, 128, 1408], P('row', 'col'), may hold values from -6.5 to 6.5
- values: bfloat16 [16, 16, 128, 1408], P('row', 'col'), may hold values from -6 to 6
- dout: bfloat16 [16, 16, 128, 1408], P('row', 'col'), may hold values from -36 to 36
- link_query: int32 [8, 16, 16], replicated, may hold values from 0 to 1
- link_key: int32 [8, 16, 16], replicated, may hold values from 0 to 1
Outputs:
- grad_queries: bfloat16 [16, 16, 128, 1408], P('row', 'col')
- grad_keys: bfloat16 [16, 16, 128, 1408], P('row', 'col')
- grad_values: bfloat16 [16, 16, 128, 1408], P('row', 'col')
All inputs are finite; a program needn't handle non-finite values.
Results may differ from a plain program's by a relative error of at most 0.015.
Values may be sent and summed in bfloat16 or wider, within the bound.
A program may use at most 256 MiB of HBM per device.

v0:
```python
import jax
import jax.numpy as jnp
from jax import lax
from jax.sharding import PartitionSpec as P

D = 1408
HEADS = 16


group_heads = 4
window_offsets = ((1, 1), (0, 1), (2, 1), (1, 0), (1, 2))
highest = lax.Precision.HIGHEST


def extended_2(cells, sides, width):
    for axis, dim in sides:
        count = lax.axis_size(axis)
        ends = count - 1
        head = lax.slice_in_dim(cells, 0, width, axis=dim)
        tail = lax.slice_in_dim(cells, cells.shape[dim] - width, cells.shape[dim], axis=dim)
        cells = jnp.concatenate(
            [
                lax.ppermute(tail, axis, [(i, (i + 1) % count) for i in range(ends)]),
                cells,
                lax.ppermute(head, axis, [((i + 1) % count, i) for i in range(ends)]),
            ],
            axis=dim,
        )
    return cells


def from_root(block, axis, owner):
    block = jnp.where(lax.axis_index(axis) == owner, block, jnp.zeros_like(block))
    return lax.psum(block, axis)


def shifted(block, axis, distance):
    devices = range(lax.axis_size(axis))
    route = [(i - distance, i) for i in devices if i - distance in devices]
    return lax.ppermute(block, axis, route)


def head_slice(source_array, group_index):
    group_span = group_heads * (D // HEADS)
    picked = lax.dynamic_slice_in_dim(
        source_array, group_index * group_span, group_span, source_array.ndim - 1
    )
    return picked.reshape(picked.shape[:-1] + (group_heads, D // HEADS))


def join_heads(stacked):
    moved_axes = jnp.moveaxis(stacked, 0, -3)
    return moved_axes.reshape(moved_axes.shape[:-3] + (D,))


def window_scores(query_group, keys_group, usable, score_scale):
    scores = (
        jnp.einsum("bqhd,bskhd->bhqsk", query_group, keys_group, preferred_element_type=jnp.float32)
        * score_scale
    )
    return jnp.where(usable[:, None, None, :, None], scores, -jnp.inf)


def random_scores(query_group, keys_group, score_scale):
    return (
        jnp.einsum("rqhd,rkhd->rhqk", query_group, keys_group, preferred_element_type=jnp.float32)
        * score_scale
    )


def shards(queries, keys, values, dout, link_query, link_key):
    rows_here, cols_here, block_size, model_width = queries.shape
    block_count = rows_here * cols_here
    score_scale = (D // HEADS) ** (-0.5)
    group_count = HEADS // group_heads
    row_index = lax.axis_index("row")
    col_index = lax.axis_index("col")
    scene_rows = rows_here * lax.axis_size("row")
    scene_cols = cols_here * lax.axis_size("col")
    local_ids = jnp.arange(block_count, dtype=jnp.int32)
    flat_queries = queries.reshape(block_count, block_size, model_width)
    flat_keys = keys.reshape(block_count, block_size, model_width)
    flat_values = values.reshape(block_count, block_size, model_width)
    flat_dout = dout.reshape(block_count, block_size, model_width)
    key_plane = lax.dynamic_index_in_dim(link_key, row_index, 0, False)
    query_pick = lax.dynamic_index_in_dim(
        lax.dynamic_index_in_dim(link_query, row_index, 0, False), col_index, 0, False
    )
    serve_pick = lax.dynamic_index_in_dim(key_plane, col_index, 1, False)
    pick_queries = jnp.take(flat_queries, query_pick, axis=0)
    pick_dout = jnp.take(flat_dout, query_pick, axis=0)
    served_keys = jnp.take(flat_keys, serve_pick, axis=0)
    served_values = jnp.take(flat_values, serve_pick, axis=0)
    query_onehot = (query_pick[:, None] == local_ids[None, :]).astype(jnp.float32)
    serve_onehot = (serve_pick[:, None] == local_ids[None, :]).astype(jnp.bfloat16)
    local_rows = local_ids // cols_here
    local_cols = local_ids % cols_here
    ext_keys, ext_values = (
        extended_2(keys, (("row", 0), ("col", 1)), 1),
        extended_2(values, (("row", 0), ("col", 1)), 1),
    )
    global_key, global_value = (
        from_root(keys[0, 0], ("row", "col"), 0),
        from_root(values[0, 0], ("row", "col"), 0),
    )
    fetched_keys, fetched_values = (
        lax.all_to_all(served_keys, "col", split_axis=0, concat_axis=0, tiled=True),
        lax.all_to_all(served_values, "col", split_axis=0, concat_axis=0, tiled=True),
    )

    def slot_stack(extended, global_block):
        pieces = [
            extended[row_shift : row_shift + rows_here, col_shift : col_shift + cols_here]
            for row_shift, col_shift in window_offsets
        ]
        pieces.append(jnp.broadcast_to(global_block, (rows_here, cols_here) + global_block.shape))
        return jnp.stack(pieces, 2).reshape((block_count, 6) + global_block.shape)

    window_keys = slot_stack(ext_keys, global_key)
    window_values = slot_stack(ext_values, global_value)
    query_rows = row_index * rows_here + local_rows
    query_cols = col_index * cols_here + local_cols
    step_rows = jnp.array([0, -1, 1, 0, 0], jnp.int32)
    step_cols = jnp.array([0, 0, 0, -1, 1], jnp.int32)
    near_rows = query_rows[:, None] + step_rows[None, :]
    near_cols = query_cols[:, None] + step_cols[None, :]
    inside = (
        (near_rows >= 0) & (near_rows < scene_rows) & (near_cols >= 0) & (near_cols < scene_cols)
    )
    usable = jnp.concatenate([inside, jnp.ones((block_count, 1), jnp.bool_)], 1)

    def all_scores(group_index):
        query_group = head_slice(flat_queries, group_index)
        keys_group = head_slice(window_keys, group_index)
        rand_query = head_slice(pick_queries, group_index)
        rand_keys = head_slice(fetched_keys, group_index)
        return (
            window_scores(query_group, keys_group, usable, score_scale),
            random_scores(rand_query, rand_keys, score_scale),
        )

    def stats_group(group_index):
        grad_out = head_slice(flat_dout, group_index)
        values_group = head_slice(window_values, group_index)
        rand_values = head_slice(fetched_values, group_index)
        scores_window, scores_random = all_scores(group_index)
        top_random = jnp.max(scores_random, axis=3)
        peak_score = jnp.maximum(
            jnp.max(scores_window, axis=(3, 4)),
            jnp.max(
                jnp.where(query_onehot[:, :, None, None] > 0, top_random[:, None], -jnp.inf), axis=0
            ),
        )
        peak_slot = jnp.take(peak_score, query_pick, axis=0)
        normalizer = jnp.sum(jnp.exp(scores_window - peak_score[..., None, None]), axis=(3, 4))
        normalizer = normalizer + jnp.einsum(
            "rb,rhq->bhq",
            query_onehot,
            jnp.sum(jnp.exp(scores_random - peak_slot[..., None]), axis=3),
            precision=highest,
        )
        log_total = peak_score + jnp.log(normalizer)
        log_slot = jnp.take(log_total, query_pick, axis=0)
        weights_window = jnp.exp(scores_window - log_total[..., None, None]).astype(jnp.bfloat16)
        weights_random = jnp.exp(scores_random - log_slot[..., None]).astype(jnp.bfloat16)
        attended = jnp.einsum(
            "bhqsk,bskhd->bqhd", weights_window, values_group, preferred_element_type=jnp.float32
        )
        random_part = jnp.einsum(
            "rhqk,rkhd->rqhd", weights_random, rand_values, preferred_element_type=jnp.float32
        )
        attended = attended + jnp.einsum(
            "rb,rqhd->bqhd", query_onehot, random_part, precision=highest
        )
        row_delta = jnp.moveaxis(jnp.sum(grad_out.astype(jnp.float32) * attended, axis=3), 1, 2)
        return (log_total, row_delta)

    log_stack, delta_stack = lax.map(stats_group, jnp.arange(group_count))

    def grads_group(group_index):
        query_group = head_slice(flat_queries, group_index)
        grad_out = head_slice(flat_dout, group_index)
        keys_group = head_slice(window_keys, group_index)
        values_group = head_slice(window_values, group_index)
        rand_query = head_slice(pick_queries, group_index)
        rand_dout = head_slice(pick_dout, group_index)
        rand_keys = head_slice(fetched_keys, group_index)
        rand_values = head_slice(fetched_values, group_index)
        log_total = log_stack[group_index]
        row_delta = delta_stack[group_index]
        log_slot = jnp.take(log_total, query_pick, axis=0)
        delta_slot = jnp.take(row_delta, query_pick, axis=0)
        scores_window, scores_random = all_scores(group_index)
        weights_window = jnp.exp(scores_window - log_total[..., None, None])
        weights_random = jnp.exp(scores_random - log_slot[..., None])
        rounded_window = weights_window.astype(jnp.bfloat16)
        rounded_random = weights_random.astype(jnp.bfloat16)
        upstream_window = jnp.einsum(
            "bqhd,bskhd->bhqsk", grad_out, values_group, preferred_element_type=jnp.float32
        )
        slopes_window = (
            score_scale * weights_window * (upstream_window - row_delta[..., None, None])
        ).astype(jnp.bfloat16)
        upstream_random = jnp.einsum(
            "rqhd,rkhd->rhqk", rand_dout, rand_values, preferred_element_type=jnp.float32
        )
        slopes_random = (
            score_scale * weights_random * (upstream_random - delta_slot[..., None])
        ).astype(jnp.bfloat16)
        query_grad = jnp.einsum(
            "bhqsk,bskhd->bqhd", slopes_window, keys_group, preferred_element_type=jnp.float32
        )
        random_part = jnp.einsum(
            "rhqk,rkhd->rqhd", slopes_random, rand_keys, preferred_element_type=jnp.float32
        )
        query_grad = query_grad + jnp.einsum(
            "rb,rqhd->bqhd", query_onehot, random_part, precision=highest
        )
        key_window = jnp.einsum(
            "bhqsk,bqhd->bskhd", slopes_window, query_group, preferred_element_type=jnp.float32
        )
        value_window = jnp.einsum(
            "bhqsk,bqhd->bskhd", rounded_window, grad_out, preferred_element_type=jnp.float32
        )
        key_random = jnp.einsum(
            "rhqk,rqhd->rkhd", slopes_random, rand_query, preferred_element_type=jnp.float32
        ).astype(jnp.bfloat16)
        value_random = jnp.einsum(
            "rhqk,rqhd->rkhd", rounded_random, rand_dout, preferred_element_type=jnp.float32
        ).astype(jnp.bfloat16)
        return (query_grad, key_window, value_window, key_random, value_random)

    results = lax.map(grads_group, jnp.arange(group_count))
    query_grad = join_heads(results[0])
    key_window = join_heads(results[1])
    value_window = join_heads(results[2])
    global_terms = (jnp.sum(key_window[:, 5], 0), jnp.sum(value_window[:, 5], 0))
    back_keys, back_values = (
        lax.all_to_all(join_heads(results[3]), "col", split_axis=0, concat_axis=0, tiled=True),
        lax.all_to_all(join_heads(results[4]), "col", split_axis=0, concat_axis=0, tiled=True),
    )

    def spread(slot_terms):
        patch_grid = slot_terms.reshape(rows_here, cols_here, 6, block_size, model_width)
        extended_sum = jnp.zeros(
            (rows_here + 2, cols_here + 2, block_size, model_width), jnp.float32
        )
        for slot_index, (row_shift, col_shift) in enumerate(window_offsets):
            extended_sum = extended_sum.at[
                row_shift : row_shift + rows_here, col_shift : col_shift + cols_here
            ].add(patch_grid[:, :, slot_index])
        return extended_sum

    key_ext = spread(key_window)
    value_ext = spread(value_window)
    key_own = key_ext[1 : rows_here + 1, 1 : cols_here + 1]
    value_own = value_ext[1 : rows_here + 1, 1 : cols_here + 1]
    for by_rows, source_row, target_row in ((1, rows_here + 1, 0), (-1, 0, rows_here - 1)):
        outgoing = (
            key_ext[source_row, 1 : cols_here + 1].astype(jnp.bfloat16),
            value_ext[source_row, 1 : cols_here + 1].astype(jnp.bfloat16),
        )
        got_key, got_value = shifted((outgoing[0], outgoing[1]), "row", by_rows)
        key_own = key_own.at[target_row].add(got_key.astype(jnp.float32))
        value_own = value_own.at[target_row].add(got_value.astype(jnp.float32))
    for by_cols, source_col, target_col in ((1, cols_here + 1, 0), (-1, 0, cols_here - 1)):
        outgoing = (
            key_ext[1 : rows_here + 1, source_col].astype(jnp.bfloat16),
            value_ext[1 : rows_here + 1, source_col].astype(jnp.bfloat16),
        )
        got_key, got_value = shifted((outgoing[0], outgoing[1]), "col", by_cols)
        key_own = key_own.at[:, target_col].add(got_key.astype(jnp.float32))
        value_own = value_own.at[:, target_col].add(got_value.astype(jnp.float32))
    random_keys = jnp.einsum(
        "rb,rtd->btd", serve_onehot, back_keys, preferred_element_type=jnp.float32
    )
    random_values = jnp.einsum(
        "rb,rtd->btd", serve_onehot, back_values, preferred_element_type=jnp.float32
    )
    key_own = key_own + random_keys.reshape(rows_here, cols_here, block_size, model_width)
    value_own = value_own + random_values.reshape(rows_here, cols_here, block_size, model_width)
    global_key_sum, global_value_sum = lax.psum((global_terms[0], global_terms[1]), ("row", "col"))
    anchor = ((row_index == 0) & (col_index == 0)).astype(jnp.float32)
    key_own = key_own.at[0, 0].add(anchor * global_key_sum)
    value_own = value_own.at[0, 0].add(anchor * global_value_sum)
    query_out = query_grad.reshape(rows_here, cols_here, block_size, model_width).astype(
        jnp.bfloat16
    )
    return (query_out, key_own.astype(jnp.bfloat16), value_own.astype(jnp.bfloat16))


def solution(mesh):
    placed = (
        P("row", "col", None, None),
        P("row", "col", None, None),
        P("row", "col", None, None),
        P("row", "col", None, None),
        P(),
        P(),
    )
    return jax.shard_map(
        shards,
        mesh=mesh,
        in_specs=placed,
        out_specs=(
            P("row", "col", None, None),
            P("row", "col", None, None),
            P("row", "col", None, None),
        ),
        check_vma=False,
    )
```

profile of v0, /device:TPU:0, one launch (start us, length us, event | category | flops | bytes accessed | tf_op | source)
XLA Modules:
  0.0 1064.0 jit_solution(14554643986516775156)
XLA Ops:
  17.2 9.8 broadcast_select_fusion.4
  27.0 8.0 all-to-all-start
  61.7 9.7 broadcast_select_fusion.6
  71.5 58.2 %all-to-all-done = bf16[16,128,1408]{2,1,0:T(8,128)(2,1)} async-done(((bf16[16,128,1408]{2,1,0:T(8,128)(2,1)}), bf16[16,128,1408]{2,1,0:T(8,128)(2,1)}, u32[]{:S(2)}, u32[]{:S(2)}) %all-to-all-start) | async-done | bytes 5767200 | tf_op jit(solution)/shard_map/all_to_all | solution.py:107
  129.7 8.5 all-to-all-start.1
  159.6 73.2 %collective-permute-done.6 = bf16[4,1,128,1408]{2,3,0,1:T(8,128)(2,1)} collective-permute-done((bf16[4,1,128,1408]{2,3,0,1:T(8,128)(2,1)}, bf16[4,1,128,1408]{2,3,0,1:T(8,128)(2,1)}, u32[]{:S(2)}, u32[]{:S(2)}) %collective-permute-start.6) | collective-permute-done | bytes 1441824 | tf_op jit(solution)/shard_map/ppermute | solution.py:23
  236.0 129.7 %all-reduce.10.cloned.1.call-done = (bf16[128,1408]{0,1:T(8,128)(2,1)}, bf16[128,1408]{0,1:T(8,128)(2,1)}) async-done(((bf16[128,1408]{0,1:T(8,128)(2,1)}, bf16[128,1408]{0,1:T(8,128)(2,1)}), (bf16[128,1408]{0,1:T(8,128)(2,1)}, bf16[128,1408]{0,1:T(8,128)(2,1)})) %all-reduce.10.cloned.1.call-update) | async-done | bytes 720912 | tf_op jit(solution)/shard_map/psum | solution.py:34
  372.9 8.2 copy.364
  381.1 8.3 copy.365
  389.4 107.0 %while.54 = (s32[]{:T(128)}, f32[4,2,4,128]{3,2,1,0:T(4,128)S(1)}, f32[4,2,4,128]{3,2,1,0:T(4,128)S(1)}, pred[2,6]{1,0:T(4,128)(4,1)S(1)}, s32[4]{0:T(128)S(1)},...) while((s32[]{:T(128)}, f32[4,2,4,128]{3,2,1,0:T(4,128)S(1)}, ...), condition=%wide.region_9.12_spmd.clone.clone, body=%wide.region_2.11_spmd.clone.clone.sunk | while | flops 680853888 | bytes 53978080 | solution.py:178
  496.4 160.7 %while.55 = (s32[]{:T(128)}, bf16[4,2,128,4,88]{2,4,3,0,1:T(8,128)(2,1)}, f32[4,2,6,128,4,88]{3,5,4,0,2,1:T(8,128)}, f32[4,2,6,128,4,88]{3,5,4,0,2,1:T(8,128)}, ...) while((s32[]{:T(128)}, ...), condition=%wide.region_11.14_spmd.clone.clone, body=%wide.region_10.13_spmd.clone.clone.sunk | while | flops 1651746048 | bytes 131271208 | solution.py:233
  657.1 8.2 copy.393
  670.6 5.8 fusion.123
  719.6 6.0 fusion.124
  741.4 12.5 %copy.373 = f32[4,3,128,1408]{3,0,2,1:T(4,128)} copy(f32[4,3,128,1408]{3,2,1,0:T(8,128)} %fusion.81) | data formatting | bytes 17301504 | tf_op jit(solution)/shard_map/scatter-add | solution.py:251
  767.4 8.3 copy.379
  775.7 7.1 all-to-all-start.2
  791.2 6.3 fusion.91
  802.1 13.3 %scatter-add.45 = f32[2,1,128,1408]{3,0,2,1:T(2,128)} dynamic-update-slice(f32[2,1,128,1408]{3,0,2,1:T(2,128)} %get-tuple-element.889, f32[1,1,128,1408]{3,0,2,1:T(1,128)S(1)} %slice_add_fusion.11, s32[]{:T(128)} %constant.631.clone.1, s32[]{:T(128)} %constant.631.clone.1, s32[]{:T(128)} %constant.631.clone.1, s32[]{:T(128)} %constant.631.clone.1) | dynamic-update-slice | bytes 1441796 | tf_op jit(solution)/shard_map/scatter-add | solution.py:264
  826.7 13.4 %scatter-add.46 = f32[2,1,128,1408]{3,0,2,1:T(2,128)S(1)} dynamic-update-slice(f32[2,1,128,1408]{3,0,2,1:T(2,128)S(1)} %copy-done.17, f32[1,1,128,1408]{3,0,2,1:T(1,128)} %slice_add_fusion.10, s32[]{:T(128)} %constant.643.clone.1, s32[]{:T(128)} %constant.631.clone.1, s32[]{:T(128)} %constant.631.clone.1, s32[]{:T(128)} %constant.631.clone.1) | dynamic-update-slice | bytes 1441796 | tf_op jit(solution)/shard_map/scatter-add | solution.py:264
  840.2 183.6 %all-reduce.8.cloned.1.call-done = (f32[128,1408]{1,0:T(8,128)}, f32[128,1408]{1,0:T(8,128)}) async-done(((f32[128,1408]{1,0:T(8,128)}, f32[128,1408]{1,0:T(8,128)}), (f32[128,1408]{1,0:T(8,128)}, f32[128,1408]{1,0:T(8,128)})) %all-reduce.8.cloned.1.call-update) | async-done | bytes 1441808 | tf_op jit(solution)/shard_map/psum | solution.py:282
  1025.9 6.1 fusion.73
  1034.8 8.4 fusion.90
  1045.0 10.3 scatter-add.49
  (444 shorter events, 432.0 us)
Async XLA Ops:
  27.0 102.7 %all-to-all-start = ((bf16[16,128,1408]{2,1,0:T(8,128)(2,1)}), bf16[16,128,1408]{2,1,0:T(8,128)(2,1)}, u32[]{:S(2)}, u32[]{:S(2)}) async-start(bf16[16,128,1408]{2,1,0:T(8,128)(2,1)} %get-tuple-element.906), calls=%async_computation | async-start | bytes 11534336 | tf_op jit(solution)/shard_map/all_to_all | solution.py:107
  35.0 330.7 %all-reduce.10.cloned.1.call-start = ((), (), s32[]{:S(2)}) async-start(), calls=%async_computation.5 | async-start | bytes 1441792 | tf_op jit(solution)/shard_map/psum | solution.py:34
  36.4 102.7 %collective-permute-start.4 = (bf16[1,1,128,1408]{2,3,0,1:T(8,128)(2,1)}, bf16[1,1,128,1408]{2,3,0,1:T(8,128)(2,1)S(1)}, u32[]{:S(2)}, u32[]{:S(2)}) collective-permute-start(bf16[1,1,128,1408]{2,3,0,1:T(8,128)(2,1)} %get-tuple-element.897), channel_id=1, source_target_pairs={{0,16},{16,32},{32,48},{48,64},{64,80},{80,96},{96,112},{1,17},{17... | collective-permute-start | bytes 1081352 | tf_op jit(solution)/shard_map/ppermute | solution.py:23
  37.9 101.2 %collective-permute-start.5 = (bf16[1,1,128,1408]{2,3,0,1:T(8,128)(2,1)}, bf16[1,1,128,1408]{2,3,0,1:T(8,128)(2,1)S(1)}, u32[]{:S(2)}, u32[]{:S(2)}) collective-permute-start(bf16[1,1,128,1408]{2,3,0,1:T(8,128)(2,1)} %get-tuple-element.895), channel_id=1, source_target_pairs={{16,0},{32,16},{48,32},{64,48},{80,64},{96,80},{112,96},{17,1},{33... | collective-permute-start | bytes 1081352 | tf_op jit(solution)/shard_map/ppermute | solution.py:25
  40.5 106.9 %collective-permute-start = (bf16[1,1,128,1408]{2,3,0,1:T(8,128)(2,1)}, bf16[1,1,128,1408]{2,3,0,1:T(8,128)(2,1)S(1)}, u32[]{:S(2)}, u32[]{:S(2)}) collective-permute-start(bf16[1,1,128,1408]{2,3,0,1:T(8,128)(2,1)} %get-tuple-element.900), channel_id=1, source_target_pairs={{0,16},{16,32},{32,48},{48,64},{64,80},{80,96},{96,112},{1,17},{17... | collective-permute-start | bytes 1081352 | tf_op jit(solution)/shard_map/ppermute | solution.py:23
  45.2 102.2 %collective-permute-start.1 = (bf16[1,1,128,1408]{2,3,0,1:T(8,128)(2,1)S(1)}, bf16[1,1,128,1408]{2,3,0,1:T(8,128)(2,1)S(1)}, u32[]{:S(2)}, u32[]{:S(2)}) collective-permute-start(bf16[1,1,128,1408]{2,3,0,1:T(8,128)(2,1)S(1)} %get-tuple-element.899), channel_id=1, source_target_pairs={{16,0},{32,16},{48,32},{64,48},{80,64},{96,80},{112,96},{17,1},{33... | collective-permute-start | bytes 1081352 | tf_op jit(solution)/shard_map/ppermute | solution.py:25
  129.7 251.4 %all-to-all-start.1 = ((bf16[16,128,1408]{2,1,0:T(8,128)(2,1)}), bf16[16,128,1408]{2,1,0:T(8,128)(2,1)}, u32[]{:S(2)}, u32[]{:S(2)}) async-start(bf16[16,128,1408]{2,1,0:T(8,128)(2,1)} %get-tuple-element.905), calls=%async_computation.1 | async-start | bytes 11534336 | tf_op jit(solution)/shard_map/all_to_all | solution.py:108
  140.5 92.3 %collective-permute-start.6 = (bf16[4,1,128,1408]{2,3,0,1:T(8,128)(2,1)}, bf16[4,1,128,1408]{2,3,0,1:T(8,128)(2,1)}, u32[]{:S(2)}, u32[]{:S(2)}) collective-permute-start(bf16[4,1,128,1408]{2,3,0,1:T(8,128)(2,1)} %pad_maximum_fusion.1), channel_id=1, source_target_pairs={{0,1},{1,2},{2,3},{3,4},{4,5},{5,6},{6,7},{7,8},{8,9},{9,10},{10,1... | collective-permute-start | bytes 4325384 | tf_op jit(solution)/shard_map/ppermute | solution.py:23
  146.1 88.9 %collective-permute-start.7 = (bf16[4,1,128,1408]{2,3,0,1:T(8,128)(2,1)}, bf16[4,1,128,1408]{2,3,0,1:T(8,128)(2,1)S(1)}, u32[]{:S(2)}, u32[]{:S(2)}) collective-permute-start(bf16[4,1,128,1408]{2,3,0,1:T(8,128)(2,1)} %pad_maximum_fusion.1), channel_id=1, source_target_pairs={{1,0},{2,1},{3,2},{4,3},{5,4},{6,5},{7,6},{8,7},{9,8},{10,9},{11,1... | collective-permute-start | bytes 4325384 | tf_op jit(solution)/shard_map/ppermute | solution.py:25
  148.7 219.0 %collective-permute-start.2 = (bf16[4,1,128,1408]{2,3,0,1:T(8,128)(2,1)}, bf16[4,1,128,1408]{2,3,0,1:T(8,128)(2,1)}, u32[]{:S(2)}, u32[]{:S(2)}) collective-permute-start(bf16[4,1,128,1408]{2,3,0,1:T(8,128)(2,1)} %pad_maximum_fusion), channel_id=1, source_target_pairs={{0,1},{1,2},{2,3},{3,4},{4,5},{5,6},{6,7},{7,8},{8,9},{9,10},{10,1... | collective-permute-start | bytes 4325384 | tf_op jit(solution)/shard_map/ppermute | solution.py:23
  154.4 215.5 %collective-permute-start.3 = (bf16[4,1,128,1408]{2,3,0,1:T(8,128)(2,1)}, bf16[4,1,128,1408]{2,3,0,1:T(8,128)(2,1)}, u32[]{:S(2)}, u32[]{:S(2)}) collective-permute-start(bf16[4,1,128,1408]{2,3,0,1:T(8,128)(2,1)} %pad_maximum_fusion), channel_id=1, source_target_pairs={{1,0},{2,1},{3,2},{4,3},{5,4},{6,5},{7,6},{8,7},{9,8},{10,9},{11,1... | collective-permute-start | bytes 4325384 | tf_op jit(solution)/shard_map/ppermute | solution.py:25
  665.2 110.4 %all-to-all-start.3 = ((bf16[16,128,1408]{2,1,0:T(8,128)(2,1)}), bf16[16,128,1408]{2,1,0:T(8,128)(2,1)}, u32[]{:S(2)}, u32[]{:S(2)}) async-start(bf16[16,128,1408]{2,1,0:T(8,128)(2,1)} %copy.393), calls=%async_computation.3 | async-start | bytes 11534336 | tf_op jit(solution)/shard_map/all_to_all | solution.py:240
  698.8 125.1 %collective-permute-start.12 = (bf16[1,128,1408]{2,1,0:T(8,128)(2,1)}, bf16[1,128,1408]{2,1,0:T(8,128)(2,1)}, u32[]{:S(2)}, u32[]{:S(2)}) collective-permute-start(bf16[1,128,1408]{2,1,0:T(8,128)(2,1)} %fusion.110), channel_id=1, source_target_pairs={{0,16},{16,32},{32,48},{48,64},{64,80},{80,96},{96,112},{1,17},{17... | collective-permute-start | bytes 1081352 | tf_op jit(solution)/shard_map/ppermute | solution.py:40
  703.5 136.6 %collective-permute-start.13 = (bf16[1,128,1408]{2,1,0:T(8,128)(2,1)}, bf16[1,128,1408]{2,1,0:T(8,128)(2,1)S(1)}, u32[]{:S(2)}, u32[]{:S(2)}) collective-permute-start(bf16[1,128,1408]{2,1,0:T(8,128)(2,1)} %fusion.111), channel_id=1, source_target_pairs={{16,0},{32,16},{48,32},{64,48},{80,64},{96,80},{112,96},{17,1},{33... | collective-permute-start | bytes 1081352 | tf_op jit(solution)/shard_map/ppermute | solution.py:40
  708.6 323.3 %collective-permute-start.14 = (bf16[2,128,1408]{2,1,0:T(8,128)(2,1)}, bf16[2,128,1408]{2,1,0:T(8,128)(2,1)}, u32[]{:S(2)}, u32[]{:S(2)}) collective-permute-start(bf16[2,128,1408]{2,1,0:T(8,128)(2,1)} %get-tuple-element.879), channel_id=1, source_target_pairs={{0,1},{1,2},{2,3},{3,4},{4,5},{5,6},{6,7},{7,8},{8,9},{9,10},{10,1... | collective-permute-start | bytes 2162696 | tf_op jit(solution)/shard_map/ppermute | solution.py:40
  713.0 319.0 %collective-permute-start.15 = (bf16[2,128,1408]{2,1,0:T(8,128)(2,1)}, bf16[2,128,1408]{2,1,0:T(8,128)(2,1)}, u32[]{:S(2)}, u32[]{:S(2)}) collective-permute-start(bf16[2,128,1408]{2,1,0:T(8,128)(2,1)} %get-tuple-element.880), channel_id=1, source_target_pairs={{1,0},{2,1},{3,2},{4,3},{5,4},{6,5},{7,6},{8,7},{9,8},{10,9},{11,1... | collective-permute-start | bytes 2162696 | tf_op jit(solution)/shard_map/ppermute | solution.py:40
  756.8 40.7 %collective-permute-start.8 = (bf16[1,128,1408]{2,0,1:T(2,128)(2,1)}, bf16[1,128,1408]{2,0,1:T(2,128)(2,1)}, u32[]{:S(2)}, u32[]{:S(2)}) collective-permute-start(bf16[1,128,1408]{2,0,1:T(2,128)(2,1)} %convert_element_type.150), channel_id=1, source_target_pairs={{0,16},{16,32},{32,48},{48,64},{64,80},{80,96},{96,112},{1,17},{17... | collective-permute-start | bytes 1081352 | tf_op jit(solution)/shard_map/ppermute | solution.py:40
  775.7 259.1 %all-to-all-start.2 = ((bf16[16,128,1408]{2,1,0:T(8,128)(2,1)}), bf16[16,128,1408]{2,1,0:T(8,128)(2,1)}, u32[]{:S(2)}, u32[]{:S(2)}) async-start(bf16[16,128,1408]{2,1,0:T(8,128)(2,1)} %copy.379), calls=%async_computation.2 | async-start | bytes 11534336 | tf_op jit(solution)/shard_map/all_to_all | solution.py:239
  782.8 241.1 %all-reduce.8.cloned.1.call-start = ((), (), s32[]{:S(2)}) async-start(), calls=%async_computation.4 | async-start | bytes 2883584 | tf_op jit(solution)/shard_map/psum | solution.py:282
  797.5 17.9 %collective-permute-start.9 = (bf16[1,128,1408]{2,0,1:T(2,128)(2,1)}, bf16[1,128,1408]{2,0,1:T(2,128)(2,1)}, u32[]{:S(2)}, u32[]{:S(2)}) collective-permute-start(bf16[1,128,1408]{2,0,1:T(2,128)(2,1)} %convert_element_type.151), channel_id=1, source_target_pairs={{16,0},{32,16},{48,32},{64,48},{80,64},{96,80},{112,96},{17,1},{33... | collective-permute-start | bytes 1081352 | tf_op jit(solution)/shard_map/ppermute | solution.py:40
  815.5 219.3 %collective-permute-start.10 = (bf16[2,128,1408]{2,0,1:T(2,128)(2,1)}, bf16[2,128,1408]{2,0,1:T(2,128)(2,1)}, u32[]{:S(2)}, u32[]{:S(2)}) collective-permute-start(bf16[2,128,1408]{2,0,1:T(2,128)(2,1)} %get-tuple-element.887), channel_id=1, source_target_pairs={{0,1},{1,2},{2,3},{3,4},{4,5},{5,6},{6,7},{7,8},{8,9},{9,10},{10,1... | collective-permute-start | bytes 2162696 | tf_op jit(solution)/shard_map/ppermute | solution.py:40
  823.9 210.9 %collective-permute-start.11 = (bf16[2,128,1408]{2,0,1:T(2,128)(2,1)}, bf16[2,128,1408]{2,0,1:T(2,128)(2,1)}, u32[]{:S(2)}, u32[]{:S(2)}) collective-permute-start(bf16[2,128,1408]{2,0,1:T(2,128)(2,1)} %get-tuple-element.888), channel_id=1, source_target_pairs={{1,0},{2,1},{3,2},{4,3},{5,4},{6,5},{7,6},{8,7},{9,8},{10,9},{11,1... | collective-permute-start | bytes 2162696 | tf_op jit(solution)/shard_map/ppermute | solution.py:40
  825.4 200.4 %copy-start.23 = (s32[16]{0:T(128)S(1)}, s32[16]{0:T(128)}, u32[]{:S(2)}) copy-start(s32[16]{0:T(128)} %copy-done.22) | copy-start | bytes 196
  1043.1 13.6 %copy-start.1 = (s32[8,16,16]{2,1,0:T(8,128)S(1)}, s32[8,16,16]{2,1,0:T(8,128)}, u32[]{:S(2)}) copy-start(s32[8,16,16]{2,1,0:T(8,128)} %param.61) | copy-start | bytes 24580
  (51 other events, 202.2 us)
Sparse Core Ops, SparseCore 0:
  46.6 319.0 all-reduce.9
  791.3 232.4 all-reduce.7
where the time goes:
time: 1080 us; the launch traced here: 1060 us
  waiting for transfers between devices  445 us (41%)
  local copies, waits for them, and re-layouts  289 us (27%)
  matrix products  144 us (13%)
  other arithmetic  84.3 us (8%)
  starting transfers between devices  72.3 us (7%)
  between operations  15 us (1%)
  loops' own time  14.2 us (1%)
    psum x1, waiting for transfers between devices, shards(): lax.psum((global_terms[0], global_terms[1]), ('row', 'col'))  184 us
    psum x1, waiting for transfers between devices, from_root(): return lax.psum(block, axis)  130 us
    dynamic_slice x40, local copies, waits for them, and re-layouts, head_slice(): lax.dynamic_slice_in_dim(source_array, group_index * group_span, group_sp...  75.4 us
    ppermute x4, waiting for transfers between devices, extended_2(): lax.ppermute(tail, axis, [(i, (i + 1) % count) for i in range(ends)])  73.2 us
    unnamed x59, local copies, waits for them, and re-layouts  61.4 us
    all_to_all x1, waiting for transfers between devices, shards(): lax.all_to_all(served_keys, 'col', split_axis=0, concat_axis=0, tiled=True)  58.2 us
    scatter-add x2, local copies, waits for them, and re-layouts, shards(): key_own = key_own.at[target_row].add(got_key.astype(jnp.float32))  26.7 us
    scatter-add x5, local copies, waits for them, and re-layouts, spread(): extended_sum = extended_sum.at[row_shift:row_shift + rows_here, col_shift...  23.7 us
  transfers between devices with their start and end apart: 22, of which 5 were waited for; matrix products, arithmetic and copies ran while one was open for 19% of the time, Pallas kernels for 0%

commit v1 on v0

v1 whole, which is shorter than its diff:
```python
import functools

import jax
import jax.numpy as jnp
from jax import lax
from jax.experimental import pallas as pl
from jax.experimental.pallas import tpu as pltpu
from jax.sharding import PartitionSpec as P

D = 1408
HEADS = 16
HD = D // HEADS
BLK = 128
ROWS = 8
COLS = 16
SIDE = 4
PAIR = 2 * HD
TILES = D // BLK
ABOVE = 2 * COLS
BELOW = 3 * COLS
GLOBAL = 4 * COLS
KEY_BLOCKS = GLOBAL + 1
WINDOW = 12
SLOTS = WINDOW + COLS
SCALE = HD ** (-0.5)
LOG2E = 1.4426950408889634
NEG = -1e30
MESH = pl.DeviceIdType.MESH
f32 = jnp.float32
bf16 = jnp.bfloat16


def moved(col, step):
    x = lax.rem(col // SIDE + step // SIDE + SIDE, SIDE)
    z = lax.rem(lax.rem(col, SIDE) + lax.rem(step, SIDE) + SIDE, SIDE)
    return x * SIDE + z


def moved_back(col, step):
    x = lax.rem(col // SIDE - step // SIDE + SIDE, SIDE)
    z = lax.rem(lax.rem(col, SIDE) - lax.rem(step, SIDE) + SIDE, SIDE)
    return x * SIDE + z


def loop(low, high, body):
    def step(i, carry):
        body(i)
        return carry

    lax.fori_loop(low, high, step, 0)


def greet(row, col):
    barrier = pltpu.get_barrier_semaphore()

    def signal_col(step):
        pl.semaphore_signal(barrier, inc=1, device_id=(row, moved(col, step)), device_id_type=MESH)

    def signal_row(step):
        pl.semaphore_signal(barrier, inc=1, device_id=(lax.rem(row + step, ROWS), col), device_id_type=MESH)

    loop(1, COLS, signal_col)
    loop(1, ROWS, signal_row)


def meet():
    pl.semaphore_wait(pltpu.get_barrier_semaphore(), COLS - 1 + ROWS - 1)


def scatter_heads(
    q_ref, k_ref, v_ref, o_ref, keys_out, query_out,
    xt_a, xt_b, send_kv, send_qo, own_sem, send_sem, recv_sem, halo_send, halo_recv, globe_send, globe_recv,
):
    row = lax.axis_index("row")
    col = lax.axis_index("col")
    up = lax.rem(row + ROWS - 1, ROWS)
    down = lax.rem(row + 1, ROWS)
    greet(row, col)

    def pack(first, second, buffer):
        def pack_block(i):
            for source, turned in ((first, xt_a), (second, xt_b)):
                for t in range(TILES):
                    span = slice(t * BLK, (t + 1) * BLK)
                    turned[span, :] = source[i, :, span].astype(f32).T
            for h in range(HEADS):
                span = slice(h * HD, (h + 1) * HD)
                buffer[h, i] = jnp.concatenate([xt_a[span, :], xt_b[span, :]], 0).astype(bf16)

        loop(0, 2, pack_block)

    def outgoing(kind, buffer, out, step):
        dest = moved(col, step)
        return pltpu.make_async_remote_copy(
            src_ref=buffer.at[dest],
            dst_ref=out.at[pl.ds(2 * col, 2)],
            send_sem=send_sem.at[kind, step],
            recv_sem=recv_sem.at[kind, step],
            device_id=(row, dest),
            device_id_type=MESH,
        )

    def incoming(kind, buffer, out, step):
        source = moved_back(col, step)
        return pltpu.make_async_remote_copy(
            src_ref=buffer.at[source],
            dst_ref=out.at[pl.ds(2 * source, 2)],
            send_sem=send_sem.at[kind, step],
            recv_sem=recv_sem.at[kind, step],
            device_id=(row, source),
            device_id_type=MESH,
        )

    def halo(way, source):
        return pltpu.make_async_remote_copy(
            src_ref=keys_out.at[2 * source + way],
            dst_ref=keys_out.at[(BELOW if way == 0 else ABOVE) + source],
            send_sem=halo_send.at[way, source],
            recv_sem=halo_recv.at[way, source],
            device_id=(up if way == 0 else down, col),
            device_id_type=MESH,
        )

    def globe(target):
        return pltpu.make_async_remote_copy(
            src_ref=keys_out.at[0],
            dst_ref=keys_out.at[GLOBAL],
            send_sem=globe_send.at[target],
            recv_sem=globe_recv.at[0],
            device_id=(target, col),
            device_id_type=MESH,
        )

    pack(k_ref, v_ref, send_kv)
    meet()
    loop(1, COLS, lambda step: outgoing(0, send_kv, keys_out, step).start())
    own_kv = pltpu.make_async_copy(send_kv.at[col], keys_out.at[pl.ds(2 * col, 2)], own_sem.at[0])
    own_kv.start()
    pack(q_ref, o_ref, send_qo)
    loop(1, COLS, lambda step: outgoing(1, send_qo, query_out, step).start())
    own_qo = pltpu.make_async_copy(send_qo.at[col], query_out.at[pl.ds(2 * col, 2)], own_sem.at[1])
    own_qo.start()
    own_kv.wait()

    def pass_on(source):
        for way in range(2):
            halo(way, source).start()

    pass_on(col)

    def landed(step):
        incoming(0, send_kv, keys_out, step).wait_recv()
        pass_on(moved_back(col, step))

    loop(1, COLS, landed)

    @pl.when(row == 0)
    def _():
        loop(1, ROWS, lambda target: globe(target).start())
        own_globe = pltpu.make_async_copy(keys_out.at[0], keys_out.at[GLOBAL], own_sem.at[2])
        own_globe.start()
        own_globe.wait()

    own_qo.wait()
    loop(1, COLS, lambda step: incoming(1, send_qo, query_out, step).wait_recv())
    loop(0, COLS, lambda source: [halo(way, source).wait_recv() for way in range(2)])

    @pl.when(row != 0)
    def _():
        globe(0).wait_recv()

    loop(1, COLS, lambda step: outgoing(0, send_kv, keys_out, step).wait_send())
    loop(1, COLS, lambda step: outgoing(1, send_qo, query_out, step).wait_send())
    loop(0, COLS, lambda source: [halo(way, source).wait_send() for way in range(2)])

    @pl.when(row == 0)
    def _():
        loop(1, ROWS, lambda target: globe(target).wait_send())


def attend(
    link_query, link_key, keys_ref, query_ref, dq_out, own_out, halo_out, globe_out,
    kvn, acc, both, both_t, p_s, u_s, m_s, l_s, a_s, f_s, delta_s, dq_s,
):
    row = lax.axis_index("row")
    factor = SCALE * LOG2E
    top_rows = lax.broadcasted_iota(jnp.int32, (PAIR, BLK), 0) < HD
    left_lanes = lax.broadcasted_iota(jnp.int32, (BLK, PAIR), 1) < HD
    scale_rows = jnp.where(top_rows, f32(SCALE), f32(1.0))

    def prepare(b):
        kvn[b] = keys_ref[b].astype(f32).T.astype(bf16)
        acc[b] = jnp.zeros((BLK, PAIR), f32)

    loop(0, KEY_BLOCKS, prepare)

    def forward(i, block, t, usable):
        su = jnp.dot(kvn[block], both[i], preferred_element_type=f32)
        s, u = su[:, :BLK], su[:, BLK:]
        m = jnp.max(s, axis=0, keepdims=True)
        p = jnp.exp2((s - m) * factor)
        p_s[t] = p
        u_s[t] = u
        m_s[i, pl.ds(t, 1), :] = m if usable is None else jnp.where(usable, m, NEG)
        l_s[i, pl.ds(t, 1), :] = jnp.sum(p, axis=0, keepdims=True)
        a_s[i, pl.ds(t, 1), :] = jnp.sum(p * u, axis=0, keepdims=True)

    def backward(i, block, t):
        w = p_s[t] * f_s[i, pl.ds(t, 1), :]
        slope = w * (u_s[t] - delta_s[i])
        slope_b = slope.astype(bf16)
        terms = jnp.concatenate([slope_b, w.astype(bf16)], 1)
        acc[block] += jnp.dot(terms, both_t[i], preferred_element_type=f32)
        return jnp.dot(keys_ref[block, :HD, :], slope_b, preferred_element_type=f32)

    def patch(c):
        left = jnp.maximum(c - 1, 0)
        right = jnp.minimum(c + 1, COLS - 1)
        window = []
        for i in range(2):
            window.append((i, 2 * c + i, None))
            window.append((i, 2 * c + 1 - i, None))
            window.append((i, (ABOVE if i == 0 else BELOW) + c, (row > 0) if i == 0 else (row < ROWS - 1)))
            window.append((i, 2 * left + i, c > 0))
            window.append((i, 2 * right + i, c < COLS - 1))
            window.append((i, GLOBAL, None))
        for i in range(2):
            pair = query_ref[2 * c + i]
            zero = jnp.zeros_like(pair)
            both[i] = jnp.concatenate([jnp.where(top_rows, pair, zero), jnp.where(top_rows, zero, pair)], 1)
            turned = pair.astype(f32).T
            none = jnp.zeros_like(turned)
            both_t[i] = jnp.concatenate(
                [jnp.where(left_lanes, turned, none), jnp.where(left_lanes, none, turned)], 0
            ).astype(bf16)
        m_s[...] = jnp.full(m_s.shape, NEG, f32)
        l_s[...] = jnp.zeros(l_s.shape, f32)
        a_s[...] = jnp.zeros(a_s.shape, f32)

        for t, (i, block, usable) in enumerate(window):
            forward(i, block, t, usable)

        def link(q):
            return link_query[row, c, q], 2 * q + link_key[row, c, q]

        def forward_links(g):
            for e in range(4):
                q = 4 * g + e
                i, block = link(q)
                forward(i, block, WINDOW + q, None)

        loop(0, COLS // 4, forward_links)

        for i in range(2):
            peak = m_s[i]
            top = jnp.max(peak, axis=0, keepdims=True)
            part = jnp.exp2((peak - top) * factor)
            inverse = 1.0 / jnp.sum(l_s[i] * part, axis=0, keepdims=True)
            delta_s[i] = jnp.sum(a_s[i] * part, axis=0, keepdims=True) * inverse
            f_s[i] = part * inverse

        for i in range(2):
            total = None
            for t, (own, block, _) in enumerate(window):
                if own == i:
                    term = backward(i, block, t)
                    total = term if total is None else total + term
            dq_s[i] = total

        def backward_links(g):
            for e in range(4):
                q = 4 * g + e
                i, block = link(q)
                dq_s[i] += backward(i, block, WINDOW + q)

        loop(0, COLS // 4, backward_links)
        dq_out[c] = (jnp.concatenate([dq_s[0], dq_s[1]], 0) * SCALE).astype(bf16)

    loop(0, COLS, patch)

    def finish_own(b):
        own_out[b] = acc[b].T * scale_rows

    def finish_halo(b):
        halo_out[b] = (acc[ABOVE + b].T * scale_rows).astype(bf16)

    loop(0, ABOVE, finish_own)
    loop(0, ABOVE, finish_halo)
    globe_out[...] = acc[GLOBAL].T * scale_rows


def gather_heads(
    dq_ref, own_ref, halo_ref, globe_ref, gq_out, gk_out, gv_out,
    got_dq, send_kv, got_kv, halo_in, globe_in, globe_sum, wide,
    own_sem, send_sem, recv_sem, halo_send, halo_recv, globe_send, globe_recv,
):
    row = lax.axis_index("row")
    col = lax.axis_index("col")
    up = lax.rem(row + ROWS - 1, ROWS)
    down = lax.rem(row + 1, ROWS)
    greet(row, col)

    def outgoing(kind, buffer, slots, step):
        dest = moved(col, step)
        return pltpu.make_async_remote_copy(
            src_ref=buffer.at[dest],
            dst_ref=slots.at[col],
            send_sem=send_sem.at[kind, step],
            recv_sem=recv_sem.at[kind, step],
            device_id=(row, dest),
            device_id_type=MESH,
        )

    def incoming(kind, buffer, slots, step):
        source = moved_back(col, step)
        return pltpu.make_async_remote_copy(
            src_ref=buffer.at[source],
            dst_ref=slots.at[source],
            send_sem=send_sem.at[kind, step],
            recv_sem=recv_sem.at[kind, step],
            device_id=(row, source),
            device_id_type=MESH,
        )

    def halo(way, c):
        return pltpu.make_async_remote_copy(
            src_ref=halo_ref.at[way * COLS + c],
            dst_ref=halo_in.at[1 - way, c],
            send_sem=halo_send.at[way, c],
            recv_sem=halo_recv.at[way, c],
            device_id=(up if way == 0 else down, col),
            device_id_type=MESH,
        )

    def globe(slot):
        return pltpu.make_async_remote_copy(
            src_ref=globe_ref,
            dst_ref=globe_in.at[slot],
            send_sem=globe_send.at[0],
            recv_sem=globe_recv.at[slot],
            device_id=(0, col),
            device_id_type=MESH,
        )

    meet()
    globe_sum[...] = jnp.zeros(globe_sum.shape, f32)

    @pl.when(row != 0)
    def _():
        globe(row).start()

    def start_halo(step):
        c = moved(col, step)
        for way in range(2):
            halo(way, c).start()

    loop(0, COLS, start_halo)
    loop(1, COLS, lambda step: outgoing(0, dq_ref, got_dq, step).start())
    own_dq = pltpu.make_async_copy(dq_ref.at[col], got_dq.at[col], own_sem.at[0])
    own_dq.start()

    @pl.when(row == 0)
    def _():
        loop(1, ROWS, lambda slot: globe(slot).wait_recv())
        total = globe_ref[...]
        for slot in range(1, ROWS):
            total = total + globe_in[slot]
        globe_sum[...] = total

    def combine(c):
        for way in range(2):
            halo(1 - way, c).wait_recv()
        for i in range(2):
            total = own_ref[2 * c + i] + halo_in[i, c].astype(f32)
            if i == 0:
                total = total + jnp.where(c == 0, globe_sum[...], 0.0)
            send_kv[c, i] = total.astype(bf16)

    def combine_and_send(step):
        combine(moved(col, step))
        outgoing(1, send_kv, got_kv, step).start()

    loop(1, COLS, combine_and_send)
    combine(col)
    own_kv = pltpu.make_async_copy(send_kv.at[col], got_kv.at[col], own_sem.at[1])
    own_kv.start()

    def unpack(i, load, out):
        for h in range(HEADS):
            wide[h * HD : (h + 1) * HD, :] = load(h)
        for t in range(TILES):
            span = slice(t * BLK, (t + 1) * BLK)
            out[i, :, span] = wide[span, :].T.astype(bf16)

    own_dq.wait()
    loop(1, COLS, lambda step: incoming(0, dq_ref, got_dq, step).wait_recv())
    for i in range(2):
        unpack(i, lambda h: got_dq[h].astype(f32)[i * HD : (i + 1) * HD], gq_out)
    own_kv.wait()
    loop(1, COLS, lambda step: incoming(1, send_kv, got_kv, step).wait_recv())

    def unpack_kv(i):
        unpack(i, lambda h: got_kv[h, i].astype(f32)[:HD], gk_out)
        unpack(i, lambda h: got_kv[h, i].astype(f32)[HD:], gv_out)

    loop(0, 2, unpack_kv)

    loop(1, COLS, lambda step: outgoing(0, dq_ref, got_dq, step).wait_send())
    loop(1, COLS, lambda step: outgoing(1, send_kv, got_kv, step).wait_send())
    loop(0, COLS, lambda c: [halo(way, c).wait_send() for way in range(2)])

    @pl.when(row != 0)
    def _():
        globe(row).wait_send()


VMEM = pl.BlockSpec(memory_space=pltpu.VMEM)
ANY = pl.BlockSpec(memory_space=pl.ANY)
SMEM = pl.BlockSpec(memory_space=pltpu.SMEM)
DMA = pltpu.SemaphoreType.DMA
LIMIT = 58 * 1024 * 1024


def shape(dims, kind):
    return jax.ShapeDtypeStruct(dims, kind)


def shards(queries, keys, values, dout, link_query, link_key):
    flat = [a.reshape(2, BLK, D) for a in (queries, keys, values, dout)]
    packed_kv, packed_q = pl.pallas_call(
        scatter_heads,
        out_shape=(shape((KEY_BLOCKS, PAIR, BLK), bf16), shape((2 * COLS, PAIR, BLK), bf16)),
        in_specs=[VMEM] * 4,
        out_specs=(ANY, ANY),
        scratch_shapes=[
            pltpu.VMEM((D, BLK), f32),
            pltpu.VMEM((D, BLK), f32),
            pltpu.VMEM((HEADS, 2, PAIR, BLK), bf16),
            pltpu.VMEM((HEADS, 2, PAIR, BLK), bf16),
            DMA((3,)),
            DMA((2, COLS)),
            DMA((2, COLS)),
            DMA((2, COLS)),
            DMA((2, COLS)),
            DMA((ROWS,)),
            DMA((1,)),
        ],
        compiler_params=pltpu.CompilerParams(collective_id=0, has_side_effects=True, vmem_limit_bytes=LIMIT),
        name="scatter_heads",
    )(*flat)
    dq, own, halo, globe = pl.pallas_call(
        attend,
        out_shape=(
            shape((COLS, PAIR, BLK), bf16),
            shape((2 * COLS, PAIR, BLK), f32),
            shape((2 * COLS, PAIR, BLK), bf16),
            shape((PAIR, BLK), f32),
        ),
        in_specs=[SMEM, SMEM, VMEM, VMEM],
        out_specs=(VMEM,) * 4,
        scratch_shapes=[
            pltpu.VMEM((KEY_BLOCKS, BLK, PAIR), bf16),
            pltpu.VMEM((KEY_BLOCKS, BLK, PAIR), f32),
            pltpu.VMEM((2, PAIR, 2 * BLK), bf16),
            pltpu.VMEM((2, 2 * BLK, PAIR), bf16),
            pltpu.VMEM((SLOTS, BLK, BLK), f32),
            pltpu.VMEM((SLOTS, BLK, BLK), f32),
            pltpu.VMEM((2, 32, BLK), f32),
            pltpu.VMEM((2, 32, BLK), f32),
            pltpu.VMEM((2, 32, BLK), f32),
            pltpu.VMEM((2, 32, BLK), f32),
            pltpu.VMEM((2, 1, BLK), f32),
            pltpu.VMEM((2, HD, BLK), f32),
        ],
        compiler_params=pltpu.CompilerParams(vmem_limit_bytes=LIMIT),
        name="attend",
    )(link_query, link_key, packed_kv, packed_q)
    outs = pl.pallas_call(
        gather_heads,
        out_shape=(shape((2, BLK, D), bf16),) * 3,
        in_specs=[VMEM] * 4,
        out_specs=(VMEM,) * 3,
        scratch_shapes=[
            pltpu.VMEM((COLS, PAIR, BLK), bf16),
            pltpu.VMEM((COLS, 2, PAIR, BLK), bf16),
            pltpu.VMEM((COLS, 2, PAIR, BLK), bf16),
            pltpu.VMEM((2, COLS, PAIR, BLK), bf16),
            pltpu.VMEM((ROWS, PAIR, BLK), f32),
            pltpu.VMEM((PAIR, BLK), f32),
            pltpu.VMEM((D, BLK), f32),
            DMA((2,)),
            DMA((2, COLS)),
            DMA((2, COLS)),
            DMA((2, COLS)),
            DMA((2, COLS)),
            DMA((1,)),
            DMA((ROWS,)),
        ],
        compiler_params=pltpu.CompilerParams(collective_id=1, has_side_effects=True, vmem_limit_bytes=LIMIT),
        name="gather_heads",
    )(dq, own, halo, globe)
    return tuple(o.reshape(2, 1, BLK, D) for o in outs)


def solution(mesh):
    tiled = P("row", "col", None, None)
    return jax.shard_map(
        shards,
        mesh=mesh,
        in_specs=(tiled,) * 4 + (P(), P()),
        out_specs=(tiled,) * 3,
        check_vma=False,
    )
```

time: 1080 us -> 166 us (0.15); the launches traced: 1060 us -> 166 us
  waiting for transfers between devices: 445 us -> 0 us
  local copies, waits for them, and re-layouts: 289 us -> 4.97 us
  Pallas kernels: 0 us -> 160 us
  matrix products: 144 us -> 0 us
  other arithmetic: 84.3 us -> 0 us
  starting transfers between devices: 72.3 us -> 0 us
  between operations: 15 us -> 0.66 us
  loops' own time: 14.2 us -> 0 us
    psum x2 -> x0, waiting for transfers between devices: 313 us -> none  [the longest x1 184 us: shards(): lax.psum((global_terms[0], global_terms[1]), ('row', 'col'))]
    pallas_call x0 -> x3, Pallas kernels: none -> 160 us  [the longest x1 70.2 us: shards(): pl.pallas_call(attend, out_shape=(shape((COLS, PAIR, BLK), bf16), shape((...]
    dot_general x70 -> x0, matrix products: 144 us -> none  [the longest x8 22.3 us: random_scores(): jnp.einsum('rqhd,rkhd->rhqk', query_group, keys_group, preferred_element_...]
    dynamic_slice x49 -> x0, local copies, waits for them, and re-layouts: 80.7 us -> none  [the longest x40 75.4 us: head_slice(): lax.dynamic_slice_in_dim(source_array, group_index * group_span, group_sp...]
    ppermute x16 -> x0, waiting for transfers between devices: 73.4 us -> none  [the longest x4 73.2 us: extended_2(): lax.ppermute(tail, axis, [(i, (i + 1) % count) for i in range(ends)])]
    scatter-add x8 -> x0, local copies, waits for them, and re-layouts: 60.7 us -> none  [the longest x2 26.7 us: shards(): key_own = key_own.at[target_row].add(got_key.astype(jnp.float32))]
    all_to_all x4 -> x0, waiting for transfers between devices: 58.2 us -> none  [the longest x1 58.2 us: shards(): lax.all_to_all(served_keys, 'col', split_axis=0, concat_axis=0, tiled=True)]
    unnamed x59 -> x5, local copies, waits for them, and re-layouts: 61.4 us -> 4.97 us
  transfers between devices with their start and end apart: 22 -> 0, of which waited for: 5 -> 0; matrix products, arithmetic and copies ran while one was open for 19% -> 0% of each run, Pallas kernels for 0% -> 0%
where the time goes in v1:
time: 166 us
  Pallas kernels  160 us (96%)
  local copies, waits for them, and re-layouts  4.97 us (3%)
    pallas_call x1, Pallas kernels, shards(): pl.pallas_call(attend, out_shape=(shape((COLS, PAIR, BLK), bf16), shape((...  70.2 us
    pallas_call x1, Pallas kernels, shards(): pl.pallas_call(scatter_heads, out_shape=(shape((KEY_BLOCKS, PAIR, BLK), b...  53.9 us
    pallas_call x1, Pallas kernels, shards(): pl.pallas_call(gather_heads, out_shape=(shape((2, BLK, D), bf16),) * 3, i...  35.8 us
    unnamed x5, local copies, waits for them, and re-layouts  4.97 us

profile of v1, /device:TPU:0, one launch (start us, length us, event | category | flops | bytes accessed | tf_op | source)
XLA Modules:
  0.0 165.5 jit_solution(8504836402029203880)
XLA Ops:
  0.6 53.9 %scatter_heads.1 = (bf16[65,176,128]{2,1,0:T(8,128)(2,1)}, bf16[32,176,128]{2,1,0:T(8,128)(2,1)}) custom-call(bf16[2,128,1408]{2,1,0:T(8,128)(2,1)} %bitcast.16, bf16[2,128,1408]{2,1,0:T(8,128)(2,1)} %bitcast.17, bf16[2,128,1408]{2,1,0:T(8,128)(2,1)} %bitcast.18, bf16[2,128,1408]{2,1,0:T(8,128)(2,1)} %bitcast.19), custom_call_target="tpu_custom_call" | custom-call | tf_op jit(solution)/shard_map/scatter_heads/pallas_call | solution.py:430
  54.5 70.2 %attend.1 = (bf16[16,176,128]{2,1,0:T(8,128)(2,1)}, f32[32,176,128]{2,1,0:T(8,128)}, bf16[32,176,128]{2,1,0:T(8,128)(2,1)}, f32[176,128]{1,0:T(8,128)}) custom-call(s32[8,16,16]{2,1,0:T(8,128)} %link_query.1, s32[8,16,16]{2,1,0:T(8,128)} %link_key.1, bf16[65,176,128]{2,1,0:T(8,128)(2,1)} %get-tuple-element.12.keys_ref, ...), custom_call_target="tpu_custom_call" | custom-call | tf_op jit(solution)/shard_map/attend/pallas_call | solution.py:451
  124.7 35.8 %gather_heads.1 = (bf16[2,128,1408]{2,1,0:T(8,128)(2,1)}, bf16[2,128,1408]{2,1,0:T(8,128)(2,1)}, bf16[2,128,1408]{2,1,0:T(8,128)(2,1)}) custom-call(bf16[16,176,128]{2,1,0:T(8,128)(2,1)} %get-tuple-element.14.dq_ref, f32[32,176,128]{2,1,0:T(8,128)} %get-tuple-element.15.own_ref, bf16[32,176,128]{2,1,0:T(8,128)(2,1)} %get-tuple-element.16.halo_ref, ...), custom_call_target="tpu_custom_call" | custom-call | tf_op jit(solution)/shard_map/gather_heads/pallas_call | solution.py:478
  160.5 0.0 copy-start
  160.5 2.1 %copy.15 = bf16[2,1,128,1408]{3,2,1,0:T(8,128)(2,1)} copy(bf16[2,1,128,1408]{3,2,1,0:T(8,128)(2,1)} %bitcast.15) | data formatting | bytes 1441792
  162.6 2.0 %copy.16 = bf16[2,1,128,1408]{3,2,1,0:T(8,128)(2,1)} copy(bf16[2,1,128,1408]{3,2,1,0:T(8,128)(2,1)} %bitcast.14) | data formatting | bytes 1441792
  164.6 0.0 copy-done
  164.6 0.9 copy.17
Async XLA Ops:
  160.5 4.1 %copy-start = (bf16[2,128,1408]{2,1,0:T(8,128)(2,1)S(1)}, bf16[2,128,1408]{2,1,0:T(8,128)(2,1)}, u32[]{:S(2)}) copy-start(bf16[2,128,1408]{2,1,0:T(8,128)(2,1)} %get-tuple-element.20) | copy-start | bytes 2162692

commit v2 on v1

v2 whole, which is shorter than its diff:
```python
import jax
import jax.numpy as jnp
from jax import lax
from jax.experimental import pallas as pl
from jax.experimental.pallas import tpu as pltpu
from jax.sharding import PartitionSpec as P

D = 1408
HEADS = 16
HD = D // HEADS
BLK = 128
ROWS = 8
COLS = 16
SIDE = 4
STRIDE = 5
PAIR = 2 * HD
TILES = D // BLK
ABOVE = 2 * COLS
BELOW = 3 * COLS
GLOBAL = 4 * COLS
KEY_BLOCKS = GLOBAL + 1
WINDOW = 12
SLOTS = WINDOW + COLS
SCALE = HD ** (-0.5)
LOG2E = 1.4426950408889634
NEG = -1e30
MESH = pl.DeviceIdType.MESH
f32 = jnp.float32
bf16 = jnp.bfloat16


def shifted(row, col, step, sign):
    core = lax.rem(row, 2)
    turn = lax.rem(step * STRIDE, COLS)
    first, second = turn // SIDE, lax.rem(turn, SIDE)
    dx = sign * (first * (1 - core) + (SIDE - second) * core)
    dz = sign * (second * (1 - core) + (SIDE - first) * core)
    x = lax.rem(col // SIDE + dx + SIDE, SIDE)
    z = lax.rem(lax.rem(col, SIDE) + dz + SIDE, SIDE)
    return x * SIDE + z


def loop(low, high, body):
    def step(i, carry):
        body(i)
        return carry

    lax.fori_loop(low, high, step, 0)


def turned_dot(a, b):
    return lax.dot_general(a, b, (((1,), (1,)), ((), ())), preferred_element_type=f32)


def attend(
    link_query, link_key, q_ref, k_ref, v_ref, o_ref, got_dq, got_kv,
    xt_a, xt_b, send_kv, send_qo, keys, query, kvn, both, pairs, p_s, u_s,
    m_s, l_s, a_s, f_s, d_s, i_s, send_dq, send_terms, halo_out, halo_in, globe_acc, globe_in,
    own_sem, send_sem, recv_sem, halo_send, halo_recv, back_send, back_recv, globe_send, globe_recv,
):
    row = lax.axis_index("row")
    col = lax.axis_index("col")
    up = lax.rem(row + ROWS - 1, ROWS)
    down = lax.rem(row + 1, ROWS)
    factor = SCALE * LOG2E

    barrier = pltpu.get_barrier_semaphore()

    def greet(dest_row, dest_col):
        pl.semaphore_signal(barrier, inc=1, device_id=(dest_row, dest_col), device_id_type=MESH)

    loop(1, COLS, lambda step: greet(row, lax.rem(col + step, COLS)))
    loop(1, ROWS, lambda step: greet(lax.rem(row + step, ROWS), col))

    def to_col(kind, source_ref, target_ref, step, sign):
        return pltpu.make_async_remote_copy(
            src_ref=source_ref,
            dst_ref=target_ref,
            send_sem=send_sem.at[kind, step],
            recv_sem=recv_sem.at[kind, step],
            device_id=(row, shifted(row, col, step, sign)),
            device_id_type=MESH,
        )

    def scatter(kind, buffer, out, step):
        return to_col(kind, buffer.at[shifted(row, col, step, 1)], out.at[pl.ds(2 * col, 2)], step, 1)

    def scattered(kind, buffer, out, step):
        source = shifted(row, col, step, -1)
        return to_col(kind, buffer.at[source], out.at[pl.ds(2 * source, 2)], step, -1)

    def gather(kind, buffer, out, step):
        return to_col(kind, buffer.at[shifted(row, col, step, 1)], out.at[col], step, 1)

    def gathered(kind, buffer, out, step):
        source = shifted(row, col, step, -1)
        return to_col(kind, buffer.at[source], out.at[source], step, -1)

    def halo(way, source):
        return pltpu.make_async_remote_copy(
            src_ref=keys.at[2 * source + way],
            dst_ref=keys.at[(BELOW if way == 0 else ABOVE) + source],
            send_sem=halo_send.at[way, source],
            recv_sem=halo_recv.at[way, source],
            device_id=(up if way == 0 else down, col),
            device_id_type=MESH,
        )

    def halo_back(way, c):
        return pltpu.make_async_remote_copy(
            src_ref=halo_out.at[way, c],
            dst_ref=halo_in.at[1 - way, c],
            send_sem=back_send.at[way, c],
            recv_sem=back_recv.at[way, c],
            device_id=(up if way == 0 else down, col),
            device_id_type=MESH,
        )

    def globe(target):
        return pltpu.make_async_remote_copy(
            src_ref=keys.at[0],
            dst_ref=keys.at[GLOBAL],
            send_sem=globe_send.at[target],
            recv_sem=globe_recv.at[0],
            device_id=(target, col),
            device_id_type=MESH,
        )

    def globe_back(slot):
        return pltpu.make_async_remote_copy(
            src_ref=globe_acc,
            dst_ref=globe_in.at[slot],
            send_sem=globe_send.at[0],
            recv_sem=globe_recv.at[slot],
            device_id=(0, col),
            device_id_type=MESH,
        )

    def pack(first, second, buffer):
        def pack_block(i):
            for source, turned in ((first, xt_a), (second, xt_b)):
                for t in range(TILES):
                    span = slice(t * BLK, (t + 1) * BLK)
                    turned[span, :] = source[i, :, span].astype(f32).T
            for h in range(HEADS):
                span = slice(h * HD, (h + 1) * HD)
                buffer[h, i] = jnp.concatenate([xt_a[span, :], xt_b[span, :]], 0).astype(bf16)

        loop(0, 2, pack_block)

    def prepare(b):
        kvn[b] = keys[b].astype(f32).T.astype(bf16)

    pack(k_ref, v_ref, send_kv)
    pl.semaphore_wait(barrier, COLS - 1 + ROWS - 1)
    loop(1, COLS, lambda step: scatter(0, send_kv, keys, step).start())
    own_kv = pltpu.make_async_copy(send_kv.at[col], keys.at[pl.ds(2 * col, 2)], own_sem.at[0])
    own_kv.start()
    pack(q_ref, o_ref, send_qo)
    loop(1, COLS, lambda step: scatter(1, send_qo, query, step).start())
    own_qo = pltpu.make_async_copy(send_qo.at[col], query.at[pl.ds(2 * col, 2)], own_sem.at[1])
    own_qo.start()
    own_kv.wait()

    def pass_on(source):
        for way in range(2):
            halo(way, source).start()
        for way in range(2):
            prepare(2 * source + way)

    pass_on(col)

    def landed(step):
        scattered(0, send_kv, keys, step).wait_recv()
        pass_on(shifted(row, col, step, -1))

    loop(1, COLS, landed)

    @pl.when(row == 0)
    def _():
        loop(1, ROWS, lambda target: globe(target).start())
        own_globe = pltpu.make_async_copy(keys.at[0], keys.at[GLOBAL], own_sem.at[2])
        own_globe.start()
        own_globe.wait()

    def halo_landed(source):
        for way in range(2):
            halo(way, source).wait_recv()
        prepare(ABOVE + source)
        prepare(BELOW + source)

    loop(0, COLS, halo_landed)

    @pl.when(row != 0)
    def _():
        globe(0).wait_recv()

    prepare(GLOBAL)
    own_qo.wait()

    top_rows = lax.broadcasted_iota(jnp.int32, (PAIR, BLK), 0) < HD
    scale_rows = jnp.where(top_rows, f32(SCALE), f32(1.0))
    globe_acc[...] = jnp.zeros(globe_acc.shape, f32)
    m_s[...] = jnp.full(m_s.shape, NEG, f32)
    l_s[...] = jnp.zeros(l_s.shape, f32)
    a_s[...] = jnp.zeros(a_s.shape, f32)
    i_s[...] = jnp.zeros(i_s.shape, f32)
    i_s[6:WINDOW, :] = jnp.ones((6, BLK), f32)
    i_s[SLOTS:, :] = jnp.full((32 - SLOTS, BLK), 2.0, f32)

    def forward(n, block, t, usable):
        su = jnp.dot(kvn[block], both[n], preferred_element_type=f32)
        s, u = su[:, :BLK], su[:, BLK:]
        m = jnp.max(s, axis=0, keepdims=True)
        p = jnp.exp2((s - m) * factor)
        p_s[t] = p
        u_s[t] = u
        m_s[t : t + 1, :] = m if usable is None else jnp.where(usable, m, NEG)
        l_s[t : t + 1, :] = jnp.sum(p, axis=0, keepdims=True)
        a_s[t : t + 1, :] = jnp.sum(p * u, axis=0, keepdims=True)

    def backward(c, block, t):
        w = p_s[t] * f_s[t : t + 1, :]
        slope = w * (u_s[t] - d_s[t : t + 1, :])
        terms = jnp.concatenate([slope, w], 1).astype(bf16)
        pairs[c, t] = terms
        return jnp.dot(keys[block, :HD, :], terms[:, :BLK], preferred_element_type=f32)

    def patch(c):
        left = jnp.maximum(c - 1, 0)
        right = jnp.minimum(c + 1, COLS - 1)
        slots = []
        for i in range(2):
            slots.append((i, 2 * c + i, None))
            slots.append((i, 2 * c + 1 - i, None))
            slots.append((i, (ABOVE if i == 0 else BELOW) + c, (row > 0) if i == 0 else (row < ROWS - 1)))
            slots.append((i, 2 * left + i, c > 0))
            slots.append((i, 2 * right + i, c < COLS - 1))
            slots.append((i, GLOBAL, None))
        for q in range(COLS):
            slots.append((link_query[row, c, q], 2 * q + link_key[row, c, q], None))
        for i in range(2):
            pair = query[2 * c + i]
            zero = jnp.zeros_like(pair)
            both[2 * c + i] = jnp.concatenate([jnp.where(top_rows, pair, zero), jnp.where(top_rows, zero, pair)], 1)
        for t, (i, block, usable) in enumerate(slots):
            forward(2 * c + i, block, t, usable)
            if t >= WINDOW:
                i_s[t : t + 1, :] = jnp.full((1, BLK), i.astype(f32), f32)

        picks, deltas, parts = [], [], []
        for i in range(2):
            pick = i_s[...] == float(i)
            peak = jnp.where(pick, m_s[...], NEG)
            top = jnp.max(peak, axis=0, keepdims=True)
            part = jnp.where(pick, jnp.exp2((peak - top) * factor), 0.0)
            inverse = 1.0 / jnp.sum(l_s[...] * part, axis=0, keepdims=True)
            picks.append(pick)
            deltas.append(jnp.sum(a_s[...] * part, axis=0, keepdims=True) * inverse)
            parts.append(part * inverse)
        f_s[...] = parts[0] + parts[1]
        d_s[...] = jnp.where(picks[0], deltas[0], deltas[1])

        totals = [jnp.zeros((HD, BLK), f32), jnp.zeros((HD, BLK), f32)]
        for t, (i, block, _) in enumerate(slots):
            term = backward(c, block, t)
            if t < WINDOW:
                totals[i] = totals[i] + term
            else:
                totals[0] = totals[0] + jnp.where(i == 0, term, 0.0)
                totals[1] = totals[1] + jnp.where(i == 0, 0.0, term)
        send_dq[c] = (jnp.concatenate(totals, 0) * SCALE).astype(bf16)
        for way in range(2):
            term = turned_dot(both[2 * c + way], pairs[c, 6 * way + 2])
            halo_out[way, c] = (term * scale_rows).astype(bf16)
            halo_back(way, c).start()
        globe_acc[...] += turned_dot(both[2 * c], pairs[c, 5]) + turned_dot(both[2 * c + 1], pairs[c, 11])

    patch(col)
    own_dq = pltpu.make_async_copy(send_dq.at[col], got_dq.at[col], own_sem.at[3])
    own_dq.start()

    def patch_landed(step):
        scattered(1, send_qo, query, step).wait_recv()
        patch(shifted(row, col, step, -1))
        to_col(2, send_dq.at[shifted(row, col, step, -1)], got_dq.at[col], step, -1).start()

    loop(1, COLS, patch_landed)
    globe_acc[...] = globe_acc[...] * scale_rows

    @pl.when(row == 0)
    def _():
        loop(1, ROWS, lambda target: globe(target).wait_send())

    @pl.when(row != 0)
    def _():
        globe_back(row).start()

    @pl.when(row == 0)
    def _():
        loop(1, ROWS, lambda slot: globe_back(slot).wait_recv())
        total = globe_acc[...]
        for slot in range(1, ROWS):
            total = total + globe_in[slot]
        globe_acc[...] = total

    def terms_of(q):
        left = jnp.maximum(q - 1, 0)
        right = jnp.minimum(q + 1, COLS - 1)
        sides = []
        for j in range(2):
            before = pairs[left, 6 * j + 4]
            after = pairs[right, 6 * j + 3]
            none = jnp.zeros_like(before)
            near = (
                turned_dot(both[2 * q + j], pairs[q, 6 * j])
                + turned_dot(both[2 * q + 1 - j], pairs[q, 6 * (1 - j) + 1])
                + turned_dot(both[2 * left + j], jnp.where(q > 0, before, none))
                + turned_dot(both[2 * right + j], jnp.where(q < COLS - 1, after, none))
            )
            sides.append(near)
        total = jnp.concatenate(sides, 1)
        for c in range(COLS):
            term = pairs[c, WINDOW + q]
            none = jnp.zeros_like(term)
            first = link_key[row, c, q] == 0
            split = jnp.concatenate([jnp.where(first, term, none), jnp.where(first, none, term)], 0)
            total = total + turned_dot(both[2 * c + link_query[row, c, q]], split)
        for j in range(2):
            halo_back(1 - j, q).wait_recv()
            own = total[:, j * BLK : (j + 1) * BLK] * scale_rows + halo_in[j, q].astype(f32)
            if j == 0:
                own = own + jnp.where((q == 0) & (row == 0), globe_acc[...], 0.0)
            send_terms[q, j] = own.astype(bf16)

    def send_back(step):
        terms_of(shifted(row, col, step, 1))
        gather(3, send_terms, got_kv, step).start()

    loop(1, COLS, send_back)
    terms_of(col)
    own_back = pltpu.make_async_copy(send_terms.at[col], got_kv.at[col], own_sem.at[4])
    own_back.start()

    own_dq.wait()
    own_back.wait()

    def last(step):
        to_col(2, send_dq.at[col], got_dq.at[shifted(row, col, step, 1)], step, 1).wait_recv()
        gathered(3, send_terms, got_kv, step).wait_recv()
        scatter(0, send_kv, keys, step).wait_send()
        scatter(1, send_qo, query, step).wait_send()
        to_col(2, send_dq.at[shifted(row, col, step, -1)], got_dq.at[col], step, -1).wait_send()
        gather(3, send_terms, got_kv, step).wait_send()

    loop(1, COLS, last)

    def last_halo(c):
        for way in range(2):
            halo(way, c).wait_send()
            halo_back(way, c).wait_send()

    loop(0, COLS, last_halo)

    @pl.when(row != 0)
    def _():
        globe_back(row).wait_send()


def unpack(got_dq, got_kv, gq_out, gk_out, gv_out, wide):
    def turn(i, load, out):
        for h in range(HEADS):
            wide[h * HD : (h + 1) * HD, :] = load(h)
        for t in range(TILES):
            span = slice(t * BLK, (t + 1) * BLK)
            out[i, :, span] = wide[span, :].T.astype(bf16)

    for i in range(2):
        turn(i, lambda h: got_dq[h].astype(f32)[i * HD : (i + 1) * HD], gq_out)
        turn(i, lambda h: got_kv[h, i].astype(f32)[:HD], gk_out)
        turn(i, lambda h: got_kv[h, i].astype(f32)[HD:], gv_out)


VMEM = pl.BlockSpec(memory_space=pltpu.VMEM)
SMEM = pl.BlockSpec(memory_space=pltpu.SMEM)
DMA = pltpu.SemaphoreType.DMA
LIMIT = 61 * 1024 * 1024


def shape(dims, kind):
    return jax.ShapeDtypeStruct(dims, kind)


SCRATCH = [
    pltpu.VMEM((D, BLK), f32),
    pltpu.VMEM((D, BLK), f32),
    pltpu.VMEM((HEADS, 2, PAIR, BLK), bf16),
    pltpu.VMEM((HEADS, 2, PAIR, BLK), bf16),
    pltpu.VMEM((KEY_BLOCKS, PAIR, BLK), bf16),
    pltpu.VMEM((2 * COLS, PAIR, BLK), bf16),
    pltpu.VMEM((KEY_BLOCKS, BLK, PAIR), bf16),
    pltpu.VMEM((2 * COLS, PAIR, 2 * BLK), bf16),
    pltpu.VMEM((COLS, SLOTS, BLK, 2 * BLK), bf16),
    pltpu.VMEM((SLOTS, BLK, BLK), f32),
    pltpu.VMEM((SLOTS, BLK, BLK), f32),
    pltpu.VMEM((32, BLK), f32),
    pltpu.VMEM((32, BLK), f32),
    pltpu.VMEM((32, BLK), f32),
    pltpu.VMEM((32, BLK), f32),
    pltpu.VMEM((32, BLK), f32),
    pltpu.VMEM((32, BLK), f32),
    pltpu.VMEM((COLS, PAIR, BLK), bf16),
    pltpu.VMEM((COLS, 2, PAIR, BLK), bf16),
    pltpu.VMEM((2, COLS, PAIR, BLK), bf16),
    pltpu.VMEM((2, COLS, PAIR, BLK), bf16),
    pltpu.VMEM((PAIR, BLK), f32),
    pltpu.VMEM((ROWS, PAIR, BLK), f32),
    DMA((5,)),
    DMA((4, COLS)),
    DMA((4, COLS)),
    DMA((2, COLS)),
    DMA((2, COLS)),
    DMA((2, COLS)),
    DMA((2, COLS)),
    DMA((ROWS,)),
    DMA((ROWS,)),
]


def shards(queries, keys, values, dout, link_query, link_key):
    flat = [a.reshape(2, BLK, D) for a in (queries, keys, values, dout)]
    got_dq, got_kv = pl.pallas_call(
        attend,
        out_shape=(shape((HEADS, PAIR, BLK), bf16), shape((HEADS, 2, PAIR, BLK), bf16)),
        in_specs=[SMEM, SMEM] + [VMEM] * 4,
        out_specs=(VMEM, VMEM),
        scratch_shapes=SCRATCH,
        compiler_params=pltpu.CompilerParams(collective_id=0, has_side_effects=True, vmem_limit_bytes=LIMIT),
        name="attend",
    )(link_query, link_key, *flat)
    outs = pl.pallas_call(
        unpack,
        out_shape=(shape((2, BLK, D), bf16),) * 3,
        in_specs=[VMEM] * 2,
        out_specs=(VMEM,) * 3,
        scratch_shapes=[pltpu.VMEM((D, BLK), f32)],
        compiler_params=pltpu.CompilerParams(vmem_limit_bytes=LIMIT),
        name="unpack",
    )(got_dq, got_kv)
    return tuple(o.reshape(2, 1, BLK, D) for o in outs)


def solution(mesh):
    tiled = P("row", "col", None, None)
    return jax.shard_map(
        shards,
        mesh=mesh,
        in_specs=(tiled,) * 4 + (P(), P()),
        out_specs=(tiled,) * 3,
        check_vma=False,
    )
```

time: 166 us -> 106 us (0.64)
  the two profiles are of different devices: /device:TPU:0 before, /device:TPU:2 now
where the time goes in v2:
time: 106 us; the launch traced here: 105 us
  Pallas kernels  105 us (99%)
    pallas_call x1, Pallas kernels, shards(): pl.pallas_call(attend, out_shape=(shape((HEADS, PAIR, BLK), bf16), shape(...  101 us
    pallas_call x1, Pallas kernels, shards(): pl.pallas_call(unpack, out_shape=(shape((2, BLK, D), bf16),) * 3, in_spec...  3.4 us

profile of v2, /device:TPU:2, one launch (start us, length us, event | category | flops | bytes accessed | tf_op | source)
XLA Modules:
  0.0 105.5 jit_solution(13990647271021529916)
XLA Ops:
  0.6 101.5 %attend.1 = (bf16[16,176,128]{2,1,0:T(8,128)(2,1)}, bf16[16,2,176,128]{3,2,1,0:T(8,128)(2,1)}) custom-call(s32[8,16,16]{2,1,0:T(8,128)} %link_query.1, s32[8,16,16]{2,1,0:T(8,128)} %link_key.1, bf16[2,128,1408]{2,1,0:T(8,128)(2,1)} %bitcast.13, bf16[2,128,1408]{2,1,0:T(8,128)(2,1)} %bitcast.14, bf16[2,128,1408]{2,1,0:T(8,128)(2,1)} %bitcast.15, ...), custom_call_target="tpu_custom_call" | custom-call | tf_op jit(solution)/shard_map/attend/pallas_call | solution.py:432
  102.1 3.4 %unpack.1 = (bf16[2,128,1408]{2,1,0:T(8,128)(2,1)}, bf16[2,128,1408]{2,1,0:T(8,128)(2,1)}, bf16[2,128,1408]{2,1,0:T(8,128)(2,1)}) custom-call(bf16[16,176,128]{2,1,0:T(8,128)(2,1)} %get-tuple-element.8.got_dq, bf16[16,2,176,128]{3,2,1,0:T(8,128)(2,1)} %get-tuple-element.9.got_kv), custom_call_target="tpu_custom_call" | custom-call | tf_op jit(solution)/shard_map/unpack/pallas_call | solution.py:441

commit v3 on v2

--- a/solution.py
+++ b/solution.py
@@ -15,10 +15,11 @@
 STRIDE = 5
 PAIR = 2 * HD
 TILES = D // BLK
-ABOVE = 2 * COLS
-BELOW = 3 * COLS
-GLOBAL = 4 * COLS
-KEY_BLOCKS = GLOBAL + 1
+ABOVE = 0
+BELOW = COLS
+GLOBAL = 2 * COLS
+EDGES = GLOBAL + 1
+AHEAD = 6
 WINDOW = 12
 SLOTS = WINDOW + COLS
 SCALE = HD ** (-0.5)
@@ -53,10 +54,10 @@
 
 
 def attend(
-    link_query, link_key, q_ref, k_ref, v_ref, o_ref, got_dq, got_kv,
-    xt_a, xt_b, send_kv, send_qo, keys, query, kvn, both, pairs, p_s, u_s,
+    link_query, link_key, q_in, k_in, v_in, o_in, got_dq, got_kv,
+    q_ref, k_ref, v_ref, o_ref, xt_a, xt_b, send_kv, send_qo, keys, edges, query, kvn, edges_n, both, pairs, p_s, u_s,
     m_s, l_s, a_s, f_s, d_s, i_s, send_dq, send_terms, halo_out, halo_in, globe_acc, globe_in,
-    own_sem, send_sem, recv_sem, halo_send, halo_recv, back_send, back_recv, globe_send, globe_recv,
+    in_sem, own_sem, send_sem, recv_sem, halo_send, halo_recv, back_send, back_recv, globe_send, globe_recv,
 ):
     row = lax.axis_index("row")
     col = lax.axis_index("col")
@@ -64,6 +65,12 @@
     down = lax.rem(row + 1, ROWS)
     factor = SCALE * LOG2E
 
+    loads = [
+        pltpu.make_async_copy(source, target, in_sem.at[n])
+        for n, (source, target) in enumerate(((k_in, k_ref), (v_in, v_ref), (q_in, q_ref), (o_in, o_ref)))
+    ]
+    for load in loads:
+        load.start()
     barrier = pltpu.get_barrier_semaphore()
 
     def greet(dest_row, dest_col):
@@ -99,7 +106,7 @@
     def halo(way, source):
         return pltpu.make_async_remote_copy(
             src_ref=keys.at[2 * source + way],
-            dst_ref=keys.at[(BELOW if way == 0 else ABOVE) + source],
+            dst_ref=edges.at[(BELOW if way == 0 else ABOVE) + source],
             send_sem=halo_send.at[way, source],
             recv_sem=halo_recv.at[way, source],
             device_id=(up if way == 0 else down, col),
@@ -119,7 +126,7 @@
     def globe(target):
         return pltpu.make_async_remote_copy(
             src_ref=keys.at[0],
-            dst_ref=keys.at[GLOBAL],
+            dst_ref=edges.at[GLOBAL],
             send_sem=globe_send.at[target],
             recv_sem=globe_recv.at[0],
             device_id=(target, col),
@@ -148,16 +155,19 @@
 
         loop(0, 2, pack_block)
 
-    def prepare(b):
-        kvn[b] = keys[b].astype(f32).T.astype(bf16)
-
+    def prepare(source, target, b):
+        target[b] = source[b].astype(f32).T.astype(bf16)
+
+    loads[0].wait()
+    loads[1].wait()
     pack(k_ref, v_ref, send_kv)
     pl.semaphore_wait(barrier, COLS - 1 + ROWS - 1)
     loop(1, COLS, lambda step: scatter(0, send_kv, keys, step).start())
     own_kv = pltpu.make_async_copy(send_kv.at[col], keys.at[pl.ds(2 * col, 2)], own_sem.at[0])
     own_kv.start()
+    loads[2].wait()
+    loads[3].wait()
     pack(q_ref, o_ref, send_qo)
-    loop(1, COLS, lambda step: scatter(1, send_qo, query, step).start())
     own_qo = pltpu.make_async_copy(send_qo.at[col], query.at[pl.ds(2 * col, 2)], own_sem.at[1])
     own_qo.start()
     own_kv.wait()
@@ -165,8 +175,19 @@
     def pass_on(source):
         for way in range(2):
             halo(way, source).start()
+
+        @pl.when((row == 0) & (source == 0))
+        def _():
+            loop(1, ROWS, lambda target: globe(target).start())
+
         for way in range(2):
-            prepare(2 * source + way)
+            prepare(keys, kvn, 2 * source + way)
+
+    def halo_landed(source):
+        for way in range(2):
+            halo(way, source).wait_recv()
+        prepare(edges, edges_n, ABOVE + source)
+        prepare(edges, edges_n, BELOW + source)
 
     pass_on(col)
 
@@ -175,27 +196,19 @@
         pass_on(shifted(row, col, step, -1))
 
     loop(1, COLS, landed)
+    loop(1, 1 + AHEAD, lambda step: scatter(1, send_qo, query, step).start())
 
     @pl.when(row == 0)
     def _():
-        loop(1, ROWS, lambda target: globe(target).start())
-        own_globe = pltpu.make_async_copy(keys.at[0], keys.at[GLOBAL], own_sem.at[2])
+        own_globe = pltpu.make_async_copy(keys.at[0], edges.at[GLOBAL], own_sem.at[2])
         own_globe.start()
         own_globe.wait()
-
-    def halo_landed(source):
-        for way in range(2):
-            halo(way, source).wait_recv()
-        prepare(ABOVE + source)
-        prepare(BELOW + source)
-
-    loop(0, COLS, halo_landed)
 
     @pl.when(row != 0)
     def _():
         globe(0).wait_recv()
 
-    prepare(GLOBAL)
+    prepare(edges, edges_n, GLOBAL)
     own_qo.wait()
 
     top_rows = lax.broadcasted_iota(jnp.int32, (PAIR, BLK), 0) < HD
@@ -208,8 +221,8 @@
     i_s[6:WINDOW, :] = jnp.ones((6, BLK), f32)
     i_s[SLOTS:, :] = jnp.full((32 - SLOTS, BLK), 2.0, f32)
 
-    def forward(n, block, t, usable):
-        su = jnp.dot(kvn[block], both[n], preferred_element_type=f32)
+    def forward(n, place, block, t, usable):
+        su = jnp.dot(place[1][block], both[n], preferred_element_type=f32)
         s, u = su[:, :BLK], su[:, BLK:]
         m = jnp.max(s, axis=0, keepdims=True)
         p = jnp.exp2((s - m) * factor)
@@ -219,32 +232,35 @@
         l_s[t : t + 1, :] = jnp.sum(p, axis=0, keepdims=True)
         a_s[t : t + 1, :] = jnp.sum(p * u, axis=0, keepdims=True)
 
-    def backward(c, block, t):
+    def backward(c, place, block, t):
         w = p_s[t] * f_s[t : t + 1, :]
         slope = w * (u_s[t] - d_s[t : t + 1, :])
         terms = jnp.concatenate([slope, w], 1).astype(bf16)
         pairs[c, t] = terms
-        return jnp.dot(keys[block, :HD, :], terms[:, :BLK], preferred_element_type=f32)
+        return jnp.dot(place[0][block, :HD, :], terms[:, :BLK], preferred_element_type=f32)
 
     def patch(c):
+        halo_landed(c)
         left = jnp.maximum(c - 1, 0)
         right = jnp.minimum(c + 1, COLS - 1)
         slots = []
+        here, edge = (keys, kvn), (edges, edges_n)
         for i in range(2):
-            slots.append((i, 2 * c + i, None))
-            slots.append((i, 2 * c + 1 - i, None))
-            slots.append((i, (ABOVE if i == 0 else BELOW) + c, (row > 0) if i == 0 else (row < ROWS - 1)))
-            slots.append((i, 2 * left + i, c > 0))
-            slots.append((i, 2 * right + i, c < COLS - 1))
-            slots.append((i, GLOBAL, None))
+            outer = (row > 0) if i == 0 else (row < ROWS - 1)
+            slots.append((i, here, 2 * c + i, None))
+            slots.append((i, here, 2 * c + 1 - i, None))
+            slots.append((i, edge, (ABOVE if i == 0 else BELOW) + c, outer))
+            slots.append((i, here, 2 * left + i, c > 0))
+            slots.append((i, here, 2 * right + i, c < COLS - 1))
+            slots.append((i, edge, GLOBAL, None))
         for q in range(COLS):
-            slots.append((link_query[row, c, q], 2 * q + link_key[row, c, q], None))
+            slots.append((link_query[row, c, q], here, 2 * q + link_key[row, c, q], None))
         for i in range(2):
             pair = query[2 * c + i]
             zero = jnp.zeros_like(pair)
             both[2 * c + i] = jnp.concatenate([jnp.where(top_rows, pair, zero), jnp.where(top_rows, zero, pair)], 1)
-        for t, (i, block, usable) in enumerate(slots):
-            forward(2 * c + i, block, t, usable)
+        for t, (i, place, block, usable) in enumerate(slots):
+            forward(2 * c + i, place, block, t, usable)
             if t >= WINDOW:
                 i_s[t : t + 1, :] = jnp.full((1, BLK), i.astype(f32), f32)
 
@@ -262,8 +278,8 @@
         d_s[...] = jnp.where(picks[0], deltas[0], deltas[1])
 
         totals = [jnp.zeros((HD, BLK), f32), jnp.zeros((HD, BLK), f32)]
-        for t, (i, block, _) in enumerate(slots):
-            term = backward(c, block, t)
+        for t, (i, place, block, _) in enumerate(slots):
+            term = backward(c, place, block, t)
             if t < WINDOW:
                 totals[i] = totals[i] + term
             else:
@@ -285,7 +301,12 @@
         patch(shifted(row, col, step, -1))
         to_col(2, send_dq.at[shifted(row, col, step, -1)], got_dq.at[col], step, -1).start()
 
-    loop(1, COLS, patch_landed)
+    def patch_and_send(step):
+        scatter(1, send_qo, query, step + AHEAD).start()
+        patch_landed(step)
+
+    loop(1, COLS - AHEAD, patch_and_send)
+    loop(COLS - AHEAD, COLS, patch_landed)
     globe_acc[...] = globe_acc[...] * scale_rows
 
     @pl.when(row == 0)
@@ -295,14 +316,6 @@
     @pl.when(row != 0)
     def _():
         globe_back(row).start()
-
-    @pl.when(row == 0)
-    def _():
-        loop(1, ROWS, lambda slot: globe_back(slot).wait_recv())
-        total = globe_acc[...]
-        for slot in range(1, ROWS):
-            total = total + globe_in[slot]
-        globe_acc[...] = total
 
     def terms_of(q):
         left = jnp.maximum(q - 1, 0)
@@ -319,26 +332,46 @@
                 + turned_dot(both[2 * right + j], jnp.where(q < COLS - 1, after, none))
             )
             sides.append(near)
-        total = jnp.concatenate(sides, 1)
         for c in range(COLS):
             term = pairs[c, WINDOW + q]
-            none = jnp.zeros_like(term)
+            term = turned_dot(both[2 * c + link_query[row, c, q]], term)
             first = link_key[row, c, q] == 0
-            split = jnp.concatenate([jnp.where(first, term, none), jnp.where(first, none, term)], 0)
-            total = total + turned_dot(both[2 * c + link_query[row, c, q]], split)
+            sides[0] = sides[0] + jnp.where(first, term, 0.0)
+            sides[1] = sides[1] + jnp.where(first, 0.0, term)
         for j in range(2):
             halo_back(1 - j, q).wait_recv()
-            own = total[:, j * BLK : (j + 1) * BLK] * scale_rows + halo_in[j, q].astype(f32)
+            own = sides[j] * scale_rows + halo_in[j, q].astype(f32)
             if j == 0:
                 own = own + jnp.where((q == 0) & (row == 0), globe_acc[...], 0.0)
             send_terms[q, j] = own.astype(bf16)
 
     def send_back(step):
-        terms_of(shifted(row, col, step, 1))
-        gather(3, send_terms, got_kv, step).start()
+        q = shifted(row, col, step, 1)
+        late = (row == 0) & (q == 0)
+        terms_of(jnp.where(late, col, q))
+
+        @pl.when(jnp.logical_not(late))
+        def _():
+            gather(3, send_terms, got_kv, step).start()
 
     loop(1, COLS, send_back)
-    terms_of(col)
+
+    @pl.when(row == 0)
+    def _():
+        loop(1, ROWS, lambda slot: globe_back(slot).wait_recv())
+        total = globe_acc[...]
+        for slot in range(1, ROWS):
+            total = total + globe_in[slot]
+        globe_acc[...] = total
+
+    terms_of(jnp.where(row == 0, 0, col))
+
+    def send_late(step):
+        @pl.when((row == 0) & (shifted(row, col, step, 1) == 0))
+        def _():
+            gather(3, send_terms, got_kv, step).start()
+
+    loop(1, COLS, send_late)
     own_back = pltpu.make_async_copy(send_terms.at[col], got_kv.at[col], own_sem.at[4])
     own_back.start()
 
@@ -382,6 +415,7 @@
 
 
 VMEM = pl.BlockSpec(memory_space=pltpu.VMEM)
+ANY = pl.BlockSpec(memory_space=pl.ANY)
 SMEM = pl.BlockSpec(memory_space=pltpu.SMEM)
 DMA = pltpu.SemaphoreType.DMA
 LIMIT = 61 * 1024 * 1024
@@ -392,13 +426,19 @@
 
 
 SCRATCH = [
+    pltpu.VMEM((2, BLK, D), bf16),
+    pltpu.VMEM((2, BLK, D), bf16),
+    pltpu.VMEM((2, BLK, D), bf16),
+    pltpu.VMEM((2, BLK, D), bf16),
     pltpu.VMEM((D, BLK), f32),
     pltpu.VMEM((D, BLK), f32),
     pltpu.VMEM((HEADS, 2, PAIR, BLK), bf16),
     pltpu.VMEM((HEADS, 2, PAIR, BLK), bf16),
-    pltpu.VMEM((KEY_BLOCKS, PAIR, BLK), bf16),
     pltpu.VMEM((2 * COLS, PAIR, BLK), bf16),
-    pltpu.VMEM((KEY_BLOCKS, BLK, PAIR), bf16),
+    pltpu.VMEM((EDGES, PAIR, BLK), bf16),
+    pltpu.VMEM((2 * COLS, PAIR, BLK), bf16),
+    pltpu.VMEM((2 * COLS, BLK, PAIR), bf16),
+    pltpu.VMEM((EDGES, BLK, PAIR), bf16),
     pltpu.VMEM((2 * COLS, PAIR, 2 * BLK), bf16),
     pltpu.VMEM((COLS, SLOTS, BLK, 2 * BLK), bf16),
     pltpu.VMEM((SLOTS, BLK, BLK), f32),
@@ -415,6 +455,7 @@
     pltpu.VMEM((2, COLS, PAIR, BLK), bf16),
     pltpu.VMEM((PAIR, BLK), f32),
     pltpu.VMEM((ROWS, PAIR, BLK), f32),
+    DMA((4,)),
     DMA((5,)),
     DMA((4, COLS)),
     DMA((4, COLS)),
@@ -432,7 +473,7 @@
     got_dq, got_kv = pl.pallas_call(
         attend,
         out_shape=(shape((HEADS, PAIR, BLK), bf16), shape((HEADS, 2, PAIR, BLK), bf16)),
-        in_specs=[SMEM, SMEM] + [VMEM] * 4,
+        in_specs=[SMEM, SMEM] + [ANY] * 4,
         out_specs=(VMEM, VMEM),
         scratch_shapes=SCRATCH,
         compiler_params=pltpu.CompilerParams(collective_id=0, has_side_effects=True, vmem_limit_bytes=LIMIT),

time: 106 us -> 96.6 us (0.911)
  the two profiles are of different devices: /device:TPU:2 before, /device:TPU:0 now
where the time goes in v3:
time: 96.6 us; the launch traced here: 96.3 us
  Pallas kernels  95.7 us (99%)
    pallas_call x1, Pallas kernels, shards(): pl.pallas_call(attend, out_shape=(shape((HEADS, PAIR, BLK), bf16), shape(...  92.3 us
    pallas_call x1, Pallas kernels, shards(): pl.pallas_call(unpack, out_shape=(shape((2, BLK, D), bf16),) * 3, in_spec...  3.4 us

profile of v3, /device:TPU:0, one launch (start us, length us, event | category | flops | bytes accessed | tf_op | source)
XLA Modules:
  0.0 96.3 jit_solution(3513509326184101713)
XLA Ops:
  0.6 92.3 %attend.1 = (bf16[16,176,128]{2,1,0:T(8,128)(2,1)}, bf16[16,2,176,128]{3,2,1,0:T(8,128)(2,1)}) custom-call(s32[8,16,16]{2,1,0:T(8,128)} %link_query.1, s32[8,16,16]{2,1,0:T(8,128)} %link_key.1, bf16[2,128,1408]{2,1,0:T(8,128)(2,1)} %bitcast.13, bf16[2,128,1408]{2,1,0:T(8,128)(2,1)} %bitcast.14, bf16[2,128,1408]{2,1,0:T(8,128)(2,1)} %bitcast.15, ...), custom_call_target="tpu_custom_call" | custom-call | tf_op jit(solution)/shard_map/attend/pallas_call | solution.py:473
  93.0 3.4 %unpack.1 = (bf16[2,128,1408]{2,1,0:T(8,128)(2,1)}, bf16[2,128,1408]{2,1,0:T(8,128)(2,1)}, bf16[2,128,1408]{2,1,0:T(8,128)(2,1)}) custom-call(bf16[16,176,128]{2,1,0:T(8,128)(2,1)} %get-tuple-element.8.got_dq, bf16[16,2,176,128]{3,2,1,0:T(8,128)(2,1)} %get-tuple-element.9.got_kv), custom_call_target="tpu_custom_call" | custom-call | tf_op jit(solution)/shard_map/unpack/pallas_call | solution.py:482

commit v4 on v3

--- a/solution.py
+++ b/solution.py
@@ -12,7 +12,7 @@
 ROWS = 8
 COLS = 16
 SIDE = 4
-STRIDE = 5
+STRIDE = 11
 PAIR = 2 * HD
 TILES = D // BLK
 ABOVE = 0
@@ -22,6 +22,7 @@
 AHEAD = 6
 WINDOW = 12
 SLOTS = WINDOW + COLS
+GROUPS = (BLK // 8, 8, BLK)
 SCALE = HD ** (-0.5)
 LOG2E = 1.4426950408889634
 NEG = -1e30
@@ -30,12 +31,10 @@
 bf16 = jnp.bfloat16
 
 
-def shifted(row, col, step, sign):
-    core = lax.rem(row, 2)
+def shifted(col, step, sign):
     turn = lax.rem(step * STRIDE, COLS)
-    first, second = turn // SIDE, lax.rem(turn, SIDE)
-    dx = sign * (first * (1 - core) + (SIDE - second) * core)
-    dz = sign * (second * (1 - core) + (SIDE - first) * core)
+    dx = sign * (turn // SIDE)
+    dz = sign * lax.rem(turn, SIDE)
     x = lax.rem(col // SIDE + dx + SIDE, SIDE)
     z = lax.rem(lax.rem(col, SIDE) + dz + SIDE, SIDE)
     return x * SIDE + z
@@ -55,8 +54,8 @@
 
 def attend(
     link_query, link_key, q_in, k_in, v_in, o_in, got_dq, got_kv,
-    q_ref, k_ref, v_ref, o_ref, xt_a, xt_b, send_kv, send_qo, keys, edges, query, kvn, edges_n, both, pairs, p_s, u_s,
-    m_s, l_s, a_s, f_s, d_s, i_s, send_dq, send_terms, halo_out, halo_in, globe_acc, globe_in,
+    first_ref, second_ref, xt_a, xt_b, send_kv, send_qo, keys, edges, query, kvn, edges_n, both, pairs, p_s, u_s,
+    m_s, l_s, a_s, f_s, d_s, send_dq, send_terms, halo_out, halo_in, globe_acc, globe_in,
     in_sem, own_sem, send_sem, recv_sem, halo_send, halo_recv, back_send, back_recv, globe_send, globe_recv,
 ):
     row = lax.axis_index("row")
@@ -67,9 +66,9 @@
 
     loads = [
         pltpu.make_async_copy(source, target, in_sem.at[n])
-        for n, (source, target) in enumerate(((k_in, k_ref), (v_in, v_ref), (q_in, q_ref), (o_in, o_ref)))
+        for n, (source, target) in enumerate(((k_in, first_ref), (v_in, second_ref), (q_in, first_ref), (o_in, second_ref)))
     ]
-    for load in loads:
+    for load in loads[:2]:
         load.start()
     barrier = pltpu.get_barrier_semaphore()
 
@@ -85,22 +84,22 @@
             dst_ref=target_ref,
             send_sem=send_sem.at[kind, step],
             recv_sem=recv_sem.at[kind, step],
-            device_id=(row, shifted(row, col, step, sign)),
+            device_id=(row, shifted(col, step, sign)),
             device_id_type=MESH,
         )
 
     def scatter(kind, buffer, out, step):
-        return to_col(kind, buffer.at[shifted(row, col, step, 1)], out.at[pl.ds(2 * col, 2)], step, 1)
+        return to_col(kind, buffer.at[shifted(col, step, 1)], out.at[pl.ds(2 * col, 2)], step, 1)
 
     def scattered(kind, buffer, out, step):
-        source = shifted(row, col, step, -1)
+        source = shifted(col, step, -1)
         return to_col(kind, buffer.at[source], out.at[pl.ds(2 * source, 2)], step, -1)
 
     def gather(kind, buffer, out, step):
-        return to_col(kind, buffer.at[shifted(row, col, step, 1)], out.at[col], step, 1)
+        return to_col(kind, buffer.at[shifted(col, step, 1)], out.at[col], step, 1)
 
     def gathered(kind, buffer, out, step):
-        source = shifted(row, col, step, -1)
+        source = shifted(col, step, -1)
         return to_col(kind, buffer.at[source], out.at[source], step, -1)
 
     def halo(way, source):
@@ -160,14 +159,16 @@
 
     loads[0].wait()
     loads[1].wait()
-    pack(k_ref, v_ref, send_kv)
+    pack(first_ref, second_ref, send_kv)
+    loads[2].start()
+    loads[3].start()
     pl.semaphore_wait(barrier, COLS - 1 + ROWS - 1)
     loop(1, COLS, lambda step: scatter(0, send_kv, keys, step).start())
     own_kv = pltpu.make_async_copy(send_kv.at[col], keys.at[pl.ds(2 * col, 2)], own_sem.at[0])
     own_kv.start()
     loads[2].wait()
     loads[3].wait()
-    pack(q_ref, o_ref, send_qo)
+    pack(first_ref, second_ref, send_qo)
     own_qo = pltpu.make_async_copy(send_qo.at[col], query.at[pl.ds(2 * col, 2)], own_sem.at[1])
     own_qo.start()
     own_kv.wait()
@@ -193,7 +194,7 @@
 
     def landed(step):
         scattered(0, send_kv, keys, step).wait_recv()
-        pass_on(shifted(row, col, step, -1))
+        pass_on(shifted(col, step, -1))
 
     loop(1, COLS, landed)
     loop(1, 1 + AHEAD, lambda step: scatter(1, send_qo, query, step).start())
@@ -214,33 +215,27 @@
     top_rows = lax.broadcasted_iota(jnp.int32, (PAIR, BLK), 0) < HD
     scale_rows = jnp.where(top_rows, f32(SCALE), f32(1.0))
     globe_acc[...] = jnp.zeros(globe_acc.shape, f32)
-    m_s[...] = jnp.full(m_s.shape, NEG, f32)
-    l_s[...] = jnp.zeros(l_s.shape, f32)
-    a_s[...] = jnp.zeros(a_s.shape, f32)
-    i_s[...] = jnp.zeros(i_s.shape, f32)
-    i_s[6:WINDOW, :] = jnp.ones((6, BLK), f32)
-    i_s[SLOTS:, :] = jnp.full((32 - SLOTS, BLK), 2.0, f32)
-
     def forward(n, place, block, t, usable):
         su = jnp.dot(place[1][block], both[n], preferred_element_type=f32)
         s, u = su[:, :BLK], su[:, BLK:]
-        m = jnp.max(s, axis=0, keepdims=True)
+        s, u = s.reshape(GROUPS), u.reshape(GROUPS)
+        m = jnp.max(s, axis=0)
         p = jnp.exp2((s - m) * factor)
         p_s[t] = p
         u_s[t] = u
-        m_s[t : t + 1, :] = m if usable is None else jnp.where(usable, m, NEG)
-        l_s[t : t + 1, :] = jnp.sum(p, axis=0, keepdims=True)
-        a_s[t : t + 1, :] = jnp.sum(p * u, axis=0, keepdims=True)
-
-    def backward(c, place, block, t):
-        w = p_s[t] * f_s[t : t + 1, :]
-        slope = w * (u_s[t] - d_s[t : t + 1, :])
-        terms = jnp.concatenate([slope, w], 1).astype(bf16)
+        m_s[t] = m if usable is None else jnp.where(usable, m, NEG)
+        l_s[t] = jnp.sum(p, axis=0)
+        a_s[t] = jnp.sum(p * u, axis=0)
+
+    def backward(c, place, block, t, half):
+        v = t + SLOTS * half
+        w = p_s[v] * f_s[v]
+        slope = w * (u_s[v] - d_s[v])
+        terms = jnp.concatenate([slope.reshape(BLK, BLK), w.reshape(BLK, BLK)], 1).astype(bf16)
         pairs[c, t] = terms
         return jnp.dot(place[0][block, :HD, :], terms[:, :BLK], preferred_element_type=f32)
 
-    def patch(c):
-        halo_landed(c)
+    def patch(c, half=0):
         left = jnp.maximum(c - 1, 0)
         right = jnp.minimum(c + 1, COLS - 1)
         slots = []
@@ -260,26 +255,38 @@
             zero = jnp.zeros_like(pair)
             both[2 * c + i] = jnp.concatenate([jnp.where(top_rows, pair, zero), jnp.where(top_rows, zero, pair)], 1)
         for t, (i, place, block, usable) in enumerate(slots):
-            forward(2 * c + i, place, block, t, usable)
-            if t >= WINDOW:
-                i_s[t : t + 1, :] = jnp.full((1, BLK), i.astype(f32), f32)
-
-        picks, deltas, parts = [], [], []
-        for i in range(2):
-            pick = i_s[...] == float(i)
-            peak = jnp.where(pick, m_s[...], NEG)
-            top = jnp.max(peak, axis=0, keepdims=True)
-            part = jnp.where(pick, jnp.exp2((peak - top) * factor), 0.0)
-            inverse = 1.0 / jnp.sum(l_s[...] * part, axis=0, keepdims=True)
-            picks.append(pick)
-            deltas.append(jnp.sum(a_s[...] * part, axis=0, keepdims=True) * inverse)
-            parts.append(part * inverse)
-        f_s[...] = parts[0] + parts[1]
-        d_s[...] = jnp.where(picks[0], deltas[0], deltas[1])
+            forward(2 * c + i, place, block, t + SLOTS * half, usable)
+
+        def of(i, here, other):
+            if isinstance(i, int):
+                return here if i == 0 else other
+            return jnp.where(i == 0, here, other)
+
+        tops = [jnp.full((8, BLK), NEG, f32)] * 2
+        for t, (i, _, _, _) in enumerate(slots):
+            m = m_s[t + SLOTS * half]
+            tops = [jnp.maximum(tops[0], of(i, m, NEG)), jnp.maximum(tops[1], of(i, NEG, m))]
+        tops = [jnp.broadcast_to(jnp.max(top, axis=0, keepdims=True), (8, BLK)) for top in tops]
+        sums, deltas = [jnp.zeros((8, BLK), f32)] * 2, [jnp.zeros((8, BLK), f32)] * 2
+        for t, (i, _, _, _) in enumerate(slots):
+            part = jnp.exp2((m_s[t + SLOTS * half] - of(i, tops[0], tops[1])) * factor)
+            f_s[t + SLOTS * half] = part
+            mass, pull = l_s[t + SLOTS * half] * part, a_s[t + SLOTS * half] * part
+            sums = [sums[0] + of(i, mass, 0.0), sums[1] + of(i, 0.0, mass)]
+            deltas = [deltas[0] + of(i, pull, 0.0), deltas[1] + of(i, 0.0, pull)]
+        inverses = [1.0 / jnp.sum(total, axis=0, keepdims=True) for total in sums]
+        deltas = [
+            jnp.broadcast_to(jnp.sum(pull, axis=0, keepdims=True) * inverse, (8, BLK))
+            for pull, inverse in zip(deltas, inverses)
+        ]
+        inverses = [jnp.broadcast_to(inverse, (8, BLK)) for inverse in inverses]
+        for t, (i, _, _, _) in enumerate(slots):
+            f_s[t + SLOTS * half] = f_s[t + SLOTS * half] * of(i, inverses[0], inverses[1])
+            d_s[t + SLOTS * half] = of(i, deltas[0], deltas[1])
 
         totals = [jnp.zeros((HD, BLK), f32), jnp.zeros((HD, BLK), f32)]
         for t, (i, place, block, _) in enumerate(slots):
-            term = backward(c, place, block, t)
+            term = backward(c, place, block, t, half)
             if t < WINDOW:
                 totals[i] = totals[i] + term
             else:
@@ -289,24 +296,41 @@
         for way in range(2):
             term = turned_dot(both[2 * c + way], pairs[c, 6 * way + 2])
             halo_out[way, c] = (term * scale_rows).astype(bf16)
-            halo_back(way, c).start()
         globe_acc[...] += turned_dot(both[2 * c], pairs[c, 5]) + turned_dot(both[2 * c + 1], pairs[c, 11])
 
+    def patch_here(step):
+        scattered(1, send_qo, query, step).wait_recv()
+        halo_landed(shifted(col, step, -1))
+
+        @pl.when(step + AHEAD < COLS)
+        def _():
+            scatter(1, send_qo, query, step + AHEAD).start()
+
+    def patch_away(step):
+        source = shifted(col, step, -1)
+        to_col(2, send_dq.at[source], got_dq.at[col], step, -1).start()
+        for way in range(2):
+            halo_back(way, source).start()
+
+    halo_landed(col)
     patch(col)
     own_dq = pltpu.make_async_copy(send_dq.at[col], got_dq.at[col], own_sem.at[3])
     own_dq.start()
-
-    def patch_landed(step):
-        scattered(1, send_qo, query, step).wait_recv()
-        patch(shifted(row, col, step, -1))
-        to_col(2, send_dq.at[shifted(row, col, step, -1)], got_dq.at[col], step, -1).start()
-
-    def patch_and_send(step):
-        scatter(1, send_qo, query, step + AHEAD).start()
-        patch_landed(step)
-
-    loop(1, COLS - AHEAD, patch_and_send)
-    loop(COLS - AHEAD, COLS, patch_landed)
+    for way in range(2):
+        halo_back(way, col).start()
+
+    def two_patches(k):
+        patch_here(2 * k + 1)
+        patch_here(2 * k + 2)
+        patch(shifted(col, 2 * k + 1, -1), 0)
+        patch(shifted(col, 2 * k + 2, -1), 1)
+        patch_away(2 * k + 1)
+        patch_away(2 * k + 2)
+
+    loop(0, COLS // 2 - 1, two_patches)
+    patch_here(COLS - 1)
+    patch(shifted(col, COLS - 1, -1))
+    patch_away(COLS - 1)
     globe_acc[...] = globe_acc[...] * scale_rows
 
     @pl.when(row == 0)
@@ -346,7 +370,7 @@
             send_terms[q, j] = own.astype(bf16)
 
     def send_back(step):
-        q = shifted(row, col, step, 1)
+        q = shifted(col, step, 1)
         late = (row == 0) & (q == 0)
         terms_of(jnp.where(late, col, q))
 
@@ -367,7 +391,7 @@
     terms_of(jnp.where(row == 0, 0, col))
 
     def send_late(step):
-        @pl.when((row == 0) & (shifted(row, col, step, 1) == 0))
+        @pl.when((row == 0) & (shifted(col, step, 1) == 0))
         def _():
             gather(3, send_terms, got_kv, step).start()
 
@@ -379,11 +403,11 @@
     own_back.wait()
 
     def last(step):
-        to_col(2, send_dq.at[col], got_dq.at[shifted(row, col, step, 1)], step, 1).wait_recv()
+        to_col(2, send_dq.at[col], got_dq.at[shifted(col, step, 1)], step, 1).wait_recv()
         gathered(3, send_terms, got_kv, step).wait_recv()
         scatter(0, send_kv, keys, step).wait_send()
         scatter(1, send_qo, query, step).wait_send()
-        to_col(2, send_dq.at[shifted(row, col, step, -1)], got_dq.at[col], step, -1).wait_send()
+        to_col(2, send_dq.at[shifted(col, step, -1)], got_dq.at[col], step, -1).wait_send()
         gather(3, send_terms, got_kv, step).wait_send()
 
     loop(1, COLS, last)
@@ -400,18 +424,31 @@
         globe_back(row).wait_send()
 
 
-def unpack(got_dq, got_kv, gq_out, gk_out, gv_out, wide):
-    def turn(i, load, out):
+def unpack(got_dq, got_kv, gq_out, gk_out, gv_out, dq, kv, wide, turned, in_sem, out_sem):
+    loads = [pltpu.make_async_copy(got_dq, dq, in_sem.at[0])]
+    loads += [pltpu.make_async_copy(got_kv.at[:, i], kv.at[i], in_sem.at[1 + i]) for i in range(2)]
+    for load in loads:
+        load.start()
+    stores = []
+
+    def turn(n, i, load, out):
         for h in range(HEADS):
-            wide[h * HD : (h + 1) * HD, :] = load(h)
+            wide[n, h * HD : (h + 1) * HD, :] = load(h)
         for t in range(TILES):
             span = slice(t * BLK, (t + 1) * BLK)
-            out[i, :, span] = wide[span, :].T.astype(bf16)
-
+            turned[n, :, span] = wide[n, span, :].T.astype(bf16)
+        stores.append(pltpu.make_async_copy(turned.at[n], out.at[i], out_sem.at[n]))
+        stores[-1].start()
+
+    loads[0].wait()
     for i in range(2):
-        turn(i, lambda h: got_dq[h].astype(f32)[i * HD : (i + 1) * HD], gq_out)
-        turn(i, lambda h: got_kv[h, i].astype(f32)[:HD], gk_out)
-        turn(i, lambda h: got_kv[h, i].astype(f32)[HD:], gv_out)
+        turn(i, i, lambda h: dq[h].astype(f32)[i * HD : (i + 1) * HD], gq_out)
+    for i in range(2):
+        loads[1 + i].wait()
+        turn(2 + 2 * i, i, lambda h: kv[i, h].astype(f32)[:HD], gk_out)
+        turn(3 + 2 * i, i, lambda h: kv[i, h].astype(f32)[HD:], gv_out)
+    for store in stores:
+        store.wait()
 
 
 VMEM = pl.BlockSpec(memory_space=pltpu.VMEM)
@@ -426,8 +463,6 @@
 
 
 SCRATCH = [
-    pltpu.VMEM((2, BLK, D), bf16),
-    pltpu.VMEM((2, BLK, D), bf16),
     pltpu.VMEM((2, BLK, D), bf16),
     pltpu.VMEM((2, BLK, D), bf16),
     pltpu.VMEM((D, BLK), f32),
@@ -441,14 +476,13 @@
     pltpu.VMEM((EDGES, BLK, PAIR), bf16),
     pltpu.VMEM((2 * COLS, PAIR, 2 * BLK), bf16),
     pltpu.VMEM((COLS, SLOTS, BLK, 2 * BLK), bf16),
-    pltpu.VMEM((SLOTS, BLK, BLK), f32),
-    pltpu.VMEM((SLOTS, BLK, BLK), f32),
-    pltpu.VMEM((32, BLK), f32),
-    pltpu.VMEM((32, BLK), f32),
-    pltpu.VMEM((32, BLK), f32),
-    pltpu.VMEM((32, BLK), f32),
-    pltpu.VMEM((32, BLK), f32),
-    pltpu.VMEM((32, BLK), f32),
+    pltpu.VMEM((2 * SLOTS,) + GROUPS, f32),
+    pltpu.VMEM((2 * SLOTS,) + GROUPS, f32),
+    pltpu.VMEM((2 * SLOTS, 8, BLK), f32),
+    pltpu.VMEM((2 * SLOTS, 8, BLK), f32),
+    pltpu.VMEM((2 * SLOTS, 8, BLK), f32),
+    pltpu.VMEM((2 * SLOTS, 8, BLK), f32),
+    pltpu.VMEM((2 * SLOTS, 8, BLK), f32),
     pltpu.VMEM((COLS, PAIR, BLK), bf16),
     pltpu.VMEM((COLS, 2, PAIR, BLK), bf16),
     pltpu.VMEM((2, COLS, PAIR, BLK), bf16),
@@ -474,7 +508,7 @@
         attend,
         out_shape=(shape((HEADS, PAIR, BLK), bf16), shape((HEADS, 2, PAIR, BLK), bf16)),
         in_specs=[SMEM, SMEM] + [ANY] * 4,
-        out_specs=(VMEM, VMEM),
+        out_specs=(ANY, ANY),
         scratch_shapes=SCRATCH,
         compiler_params=pltpu.CompilerParams(collective_id=0, has_side_effects=True, vmem_limit_bytes=LIMIT),
         name="attend",
@@ -482,9 +516,16 @@
     outs = pl.pallas_call(
         unpack,
         out_shape=(shape((2, BLK, D), bf16),) * 3,
-        in_specs=[VMEM] * 2,
-        out_specs=(VMEM,) * 3,
-        scratch_shapes=[pltpu.VMEM((D, BLK), f32)],
+        in_specs=[ANY] * 2,
+        out_specs=(ANY,) * 3,
+        scratch_shapes=[
+            pltpu.VMEM((HEADS, PAIR, BLK), bf16),
+            pltpu.VMEM((2, HEADS, PAIR, BLK), bf16),
+            pltpu.VMEM((6, D, BLK), f32),
+            pltpu.VMEM((6, BLK, D), bf16),
+            DMA((3,)),
+            DMA((6,)),
+        ],
         compiler_params=pltpu.CompilerParams(vmem_limit_bytes=LIMIT),
         name="unpack",
     )(got_dq, got_kv)

time: 96.6 us -> 90.6 us (0.938)
  Pallas kernels: 95.7 us -> 89.7 us
    pallas_call x1, Pallas kernels: 92.3 us -> 87 us  [shards(): pl.pallas_call(attend, out_shape=(shape((HEADS, PAIR, BLK), bf16), shape(...]
where the time goes in v4:
time: 90.6 us; the launch traced here: 90.4 us
  Pallas kernels  89.7 us (99%)
    pallas_call x1, Pallas kernels, shards(): pl.pallas_call(attend, out_shape=(shape((HEADS, PAIR, BLK), bf16), shape(...  87 us
    pallas_call x1, Pallas kernels, shards(): pl.pallas_call(unpack, out_shape=(shape((2, BLK, D), bf16),) * 3, in_spec...  2.77 us

profile of v4, /device:TPU:0, one launch (start us, length us, event | category | flops | bytes accessed | tf_op | source)
XLA Modules:
  0.0 90.4 jit_solution(8055473136237925941)
XLA Ops:
  0.6 87.0 %attend.1 = (bf16[16,176,128]{2,1,0:T(8,128)(2,1)}, bf16[16,2,176,128]{3,2,1,0:T(8,128)(2,1)}) custom-call(s32[8,16,16]{2,1,0:T(8,128)} %link_query.1, s32[8,16,16]{2,1,0:T(8,128)} %link_key.1, bf16[2,128,1408]{2,1,0:T(8,128)(2,1)} %bitcast.13, bf16[2,128,1408]{2,1,0:T(8,128)(2,1)} %bitcast.14, bf16[2,128,1408]{2,1,0:T(8,128)(2,1)} %bitcast.15, ...), custom_call_target="tpu_custom_call" | custom-call | tf_op jit(solution)/shard_map/attend/pallas_call | solution.py:507
  87.6 2.8 %unpack.1 = (bf16[2,128,1408]{2,1,0:T(8,128)(2,1)}, bf16[2,128,1408]{2,1,0:T(8,128)(2,1)}, bf16[2,128,1408]{2,1,0:T(8,128)(2,1)}) custom-call(bf16[16,176,128]{2,1,0:T(8,128)(2,1)} %get-tuple-element.8.got_dq, bf16[16,2,176,128]{3,2,1,0:T(8,128)(2,1)} %get-tuple-element.9.got_kv), custom_call_target="tpu_custom_call" | custom-call | tf_op jit(solution)/shard_map/unpack/pallas_call | solution.py:516

commit v5 on v4

--- a/solution.py
+++ b/solution.py
@@ -88,6 +88,13 @@
             device_id_type=MESH,
         )
 
+    def scatter_key(way, step):
+        return to_col(4 * way, send_kv.at[shifted(col, step, 1), way], keys.at[2 * col + way], step, 1)
+
+    def scattered_key(way, step):
+        source = shifted(col, step, -1)
+        return to_col(4 * way, send_kv.at[source, way], keys.at[2 * source + way], step, -1)
+
     def scatter(kind, buffer, out, step):
         return to_col(kind, buffer.at[shifted(col, step, 1)], out.at[pl.ds(2 * col, 2)], step, 1)
 
@@ -163,7 +170,8 @@
     loads[2].start()
     loads[3].start()
     pl.semaphore_wait(barrier, COLS - 1 + ROWS - 1)
-    loop(1, COLS, lambda step: scatter(0, send_kv, keys, step).start())
+    for way in range(2):
+        loop(1, COLS, lambda step: scatter_key(way, step).start())
     own_kv = pltpu.make_async_copy(send_kv.at[col], keys.at[pl.ds(2 * col, 2)], own_sem.at[0])
     own_kv.start()
     loads[2].wait()
@@ -173,16 +181,15 @@
     own_qo.start()
     own_kv.wait()
 
-    def pass_on(source):
-        for way in range(2):
-            halo(way, source).start()
-
-        @pl.when((row == 0) & (source == 0))
-        def _():
-            loop(1, ROWS, lambda target: globe(target).start())
-
-        for way in range(2):
-            prepare(keys, kvn, 2 * source + way)
+    def pass_on(way, source):
+        halo(way, source).start()
+        if way == 0:
+
+            @pl.when((row == 0) & (source == 0))
+            def _():
+                loop(1, ROWS, lambda target: globe(target).start())
+
+        prepare(keys, kvn, 2 * source + way)
 
     def halo_landed(source):
         for way in range(2):
@@ -190,13 +197,15 @@
         prepare(edges, edges_n, ABOVE + source)
         prepare(edges, edges_n, BELOW + source)
 
-    pass_on(col)
-
-    def landed(step):
-        scattered(0, send_kv, keys, step).wait_recv()
-        pass_on(shifted(col, step, -1))
-
-    loop(1, COLS, landed)
+    for way in range(2):
+        pass_on(way, col)
+
+        def landed(step):
+            scattered_key(way, step).wait_recv()
+            pass_on(way, shifted(col, step, -1))
+
+        loop(1, COLS, landed)
+
     loop(1, 1 + AHEAD, lambda step: scatter(1, send_qo, query, step).start())
 
     @pl.when(row == 0)
@@ -405,7 +414,8 @@
     def last(step):
         to_col(2, send_dq.at[col], got_dq.at[shifted(col, step, 1)], step, 1).wait_recv()
         gathered(3, send_terms, got_kv, step).wait_recv()
-        scatter(0, send_kv, keys, step).wait_send()
+        for way in range(2):
+            scatter_key(way, step).wait_send()
         scatter(1, send_qo, query, step).wait_send()
         to_col(2, send_dq.at[shifted(col, step, -1)], got_dq.at[col], step, -1).wait_send()
         gather(3, send_terms, got_kv, step).wait_send()
@@ -491,8 +501,8 @@
     pltpu.VMEM((ROWS, PAIR, BLK), f32),
     DMA((4,)),
     DMA((5,)),
-    DMA((4, COLS)),
-    DMA((4, COLS)),
+    DMA((5, COLS)),
+    DMA((5, COLS)),
     DMA((2, COLS)),
     DMA((2, COLS)),
     DMA((2, COLS)),

time: 90.6 us -> 90.2 us (level)
  no operation moved by 1% of the time
where the time goes in v5:
time: 90.2 us; the launch traced here: 89.9 us
  Pallas kernels  89.3 us (99%)
    pallas_call x1, Pallas kernels, shards(): pl.pallas_call(attend, out_shape=(shape((HEADS, PAIR, BLK), bf16), shape(...  86.5 us
    pallas_call x1, Pallas kernels, shards(): pl.pallas_call(unpack, out_shape=(shape((2, BLK, D), bf16),) * 3, in_spec...  2.77 us

profile of v5, /device:TPU:0, one launch (start us, length us, event | category | flops | bytes accessed | tf_op | source)
XLA Modules:
  0.0 89.9 jit_solution(16980373519547592172)
XLA Ops:
  0.6 86.5 %attend.1 = (bf16[16,176,128]{2,1,0:T(8,128)(2,1)}, bf16[16,2,176,128]{3,2,1,0:T(8,128)(2,1)}) custom-call(s32[8,16,16]{2,1,0:T(8,128)} %link_query.1, s32[8,16,16]{2,1,0:T(8,128)} %link_key.1, bf16[2,128,1408]{2,1,0:T(8,128)(2,1)} %bitcast.13, bf16[2,128,1408]{2,1,0:T(8,128)(2,1)} %bitcast.14, bf16[2,128,1408]{2,1,0:T(8,128)(2,1)} %bitcast.15, ...), custom_call_target="tpu_custom_call" | custom-call | tf_op jit(solution)/shard_map/attend/pallas_call | solution.py:517
  87.2 2.8 %unpack.1 = (bf16[2,128,1408]{2,1,0:T(8,128)(2,1)}, bf16[2,128,1408]{2,1,0:T(8,128)(2,1)}, bf16[2,128,1408]{2,1,0:T(8,128)(2,1)}) custom-call(bf16[16,176,128]{2,1,0:T(8,128)(2,1)} %get-tuple-element.8.got_dq, bf16[16,2,176,128]{3,2,1,0:T(8,128)(2,1)} %get-tuple-element.9.got_kv), custom_call_target="tpu_custom_call" | custom-call | tf_op jit(solution)/shard_map/unpack/pallas_call | solution.py:526
